TPU v7x, 32 devices: a whole 2x2x4 slice. The times are simulated.
32 devices in a mesh: stream: 2 (over y), dp: 16 (over z, x, core).
Axes of the slice: x: 2, y: 2, z: 4, core: 2. Of those that a mesh axis runs over, the one named last changes fastest.
Arguments:
- tokens: bfloat16 [2, 256, 36, 768], P('stream', 'dp'), may hold values from -6 to 6
- region_mask: int32 [256, 36], P('dp'), may hold values from 0 to 1, as said below
- cotangent: bfloat16 [2, 256, 36, 768], P('stream', 'dp'), may hold values from -6 to 6
- cross_qkv: bfloat16 [768, 2304], replicated, may hold values from -0.21875 to 0.21875
- cross_q_bias: float32 [768], replicated, may hold values from -1.75 to 1.75
- cross_v_bias: float32 [768], replicated, may hold values from -1.75 to 1.75
- cross_out: bfloat16 [768, 768], replicated, may hold values from -0.875 to 0.875
- cross_out_bias: float32 [768], replicated, may hold values from -1.75 to 1.75
- cross_gain: float32 [768], replicated, may hold values from 0.5 to 1.5
- cross_shift: float32 [768], replicated, may hold values from -1.75 to 1.75
- self_qkv: bfloat16 [2, 768, 2304], P('stream'), may hold values from -0.21875 to 0.21875
- self_q_bias: float32 [2, 768], P('stream'), may hold values from -1.75 to 1.75
- self_v_bias: float32 [2, 768], P('stream'), may hold values from -1.75 to 1.75
- self_out: bfloat16 [2, 768, 768], P('stream'), may hold values from -0.875 to 0.875
- self_out_bias: float32 [2, 768], P('stream'), may hold values from -1.75 to 1.75
- self_gain: float32 [2, 768], P('stream'), may hold values from 0.5 to 1.5
- self_shift: float32 [2, 768], P('stream'), may hold values from -1.75 to 1.75
- ffn_in: bfloat16 [2, 768, 3072], P('stream'), may hold values from -0.21875 to 0.21875
- ffn_in_bias: float32 [2, 3072], P('stream'), may hold values from -1.75 to 1.75
- ffn_out: bfloat16 [2, 3072, 768], P('stream'), may hold values from -0.21875 to 0.21875
- ffn_out_bias: float32 [2, 768], P('stream'), may hold values from -1.75 to 1.75
- ffn_gain: float32 [2, 768], P('stream'), may hold values from 0.5 to 1.5
- ffn_shift: float32 [2, 768], P('stream'), may hold values from -1.75 to 1.75
Outputs:
- stream_out: bfloat16 [2, 256, 36, 768], P('stream', 'dp')
- tokens_grad: float32 [2, 256, 36, 768], P('stream', 'dp')
- cross_qkv_grad: float32 [768, 2304], P('dp')
- cross_q_bias_grad: float32 [768], P('dp')
- cross_v_bias_grad: float32 [768], P('dp')
- cross_out_grad: float32 [768, 768], P('dp')
- cross_out_bias_grad: float32 [768], P('dp')
- cross_gain_grad: float32 [768], P('dp')
- cross_shift_grad: float32 [768], P('dp')
- self_qkv_grad: float32 [2, 768, 2304], P('stream', 'dp')
- self_q_bias_grad: float32 [2, 768], P('stream', 'dp')
- self_v_bias_grad: float32 [2, 768], P('stream', 'dp')
- self_out_grad: float32 [2, 768, 768], P('stream', 'dp')
- self_out_bias_grad: float32 [2, 768], P('stream', 'dp')
- self_gain_grad: float32 [2, 768], P('stream', 'dp')
- self_shift_grad: float32 [2, 768], P('stream', 'dp')
- ffn_in_grad: float32 [2, 768, 3072], P('stream', 'dp')
- ffn_in_bias_grad: float32 [2, 3072], P('stream', 'dp')
- ffn_out_grad: float32 [2, 3072, 768], P('stream', 'dp')
- ffn_out_bias_grad: float32 [2, 768], P('stream', 'dp')
- ffn_gain_grad: float32 [2, 768], P('stream', 'dp')
- ffn_shift_grad: float32 [2, 768], P('stream', 'dp')
Inputs may be any that keep to these rules, and one draw needn't show every extreme that they name: `region_mask`: each row is ones in its first positions and zeros after, with 10 to 36 ones; in every block of 16 items one item, drawn from the seed, has 36.
All inputs are finite; a program needn't handle non-finite values.
Results may differ from a plain program's by a relative error of at most 0.023.
Values may be sent and summed in bfloat16 or wider, within the bound.
A program may use at most 192 MiB of HBM per device.

v0:
```python
from functools import partial

import jax
import jax.numpy as jnp
from jax import lax
from jax.sharding import PartitionSpec as P

D = 768
H = 12
HD = 64
LW = 20
LR = 36


def partner(block, axis, apart):
    count = lax.axis_size(axis)
    route = []
    for low in range(count):
        high = low | 1 << apart
        if high != low and high < count:
            route += [(low, high), (high, low)]
    return lax.ppermute(block, axis, route)


def layer_norm(row_block, norm_gain, norm_shift):
    centre = row_block - jnp.mean(row_block, axis=-1, keepdims=True)
    spread = jnp.mean(centre * centre, axis=-1, keepdims=True)
    return centre * lax.rsqrt(spread + 1e-12) * norm_gain + norm_shift


def norm_back(row_block, norm_gain, norm_shift, grad_rows):
    unused, pullback = jax.vjp(layer_norm, row_block, norm_gain, norm_shift)
    return pullback(grad_rows)


def project(low_rows, weight, q_bias, v_bias):
    projected = jnp.dot(low_rows, weight, preferred_element_type=jnp.float32)
    query_rows = (projected[:, :D] + q_bias).astype(jnp.bfloat16)
    key_rows = projected[:, D : 2 * D].astype(jnp.bfloat16)
    value_rows = (projected[:, 2 * D :] + v_bias).astype(jnp.bfloat16)
    return (query_rows, key_rows, value_rows)


def linear_back(low_rows, weight, grad_low):
    grad_rows = jnp.einsum("ne,de->nd", grad_low, weight, preferred_element_type=jnp.float32)
    grad_weight = jnp.einsum("nd,ne->de", low_rows, grad_low, preferred_element_type=jnp.float32)
    grad_bias = jnp.sum(grad_low.astype(jnp.float32), axis=0)
    return (grad_rows, grad_weight, grad_bias)


def project_back(low_rows, weight, grad_query, grad_key, grad_value):
    grad_all = jnp.concatenate([grad_query, grad_key, grad_value], axis=1)
    grad_rows = jnp.einsum("ne,de->nd", grad_all, weight, preferred_element_type=jnp.float32)
    grad_weight = jnp.einsum("nd,ne->de", low_rows, grad_all, preferred_element_type=jnp.float32)
    grad_qbias = jnp.sum(grad_query.astype(jnp.float32), axis=0)
    grad_vbias = jnp.sum(grad_value.astype(jnp.float32), axis=0)
    return (grad_rows, grad_weight, grad_qbias, grad_vbias)


def split_heads(row_block):
    return row_block.reshape(row_block.shape[0] // LR, LR, H, HD)


def masked_scores(query_heads, key_heads, key_mask):
    scores = jnp.einsum(
        "bqhd,bkhd->bhqk", query_heads, key_heads, preferred_element_type=jnp.float32
    ) * (1.0 / HD**0.5)
    return jnp.where(key_mask[:, None, None, :] > 0, scores, -1000000000.0)


def attend_forward(query_rows, key_rows, value_rows, key_mask):
    scores = masked_scores(split_heads(query_rows), split_heads(key_rows), key_mask)
    peak_score = jnp.max(scores, axis=-1, keepdims=True)
    exponent = jnp.exp(scores - peak_score)
    row_total = jnp.sum(exponent, axis=-1, keepdims=True)
    probability = (exponent / row_total).astype(jnp.bfloat16)
    attended = jnp.einsum(
        "bhqk,bkhd->bqhd", probability, split_heads(value_rows), preferred_element_type=jnp.float32
    )
    return (
        attended.reshape(query_rows.shape).astype(jnp.bfloat16),
        peak_score + jnp.log(row_total),
    )


def attend_back(query_rows, key_rows, value_rows, key_mask, log_total, grad_low):
    query_heads = split_heads(query_rows)
    key_heads = split_heads(key_rows)
    value_heads = split_heads(value_rows)
    grad_heads = split_heads(grad_low)
    probability = jnp.exp(masked_scores(query_heads, key_heads, key_mask) - log_total)
    grad_value = jnp.einsum(
        "bhqk,bqhd->bkhd",
        probability.astype(jnp.bfloat16),
        grad_heads,
        preferred_element_type=jnp.float32,
    )
    grad_prob = jnp.einsum(
        "bqhd,bkhd->bhqk", grad_heads, value_heads, preferred_element_type=jnp.float32
    )
    grad_scores = probability * (
        grad_prob - jnp.sum(grad_prob * probability, axis=-1, keepdims=True)
    )
    grad_scores = grad_scores.astype(jnp.bfloat16)
    grad_query = jnp.einsum(
        "bhqk,bkhd->bqhd", grad_scores, key_heads, preferred_element_type=jnp.float32
    ) * (1.0 / HD**0.5)
    grad_key = jnp.einsum(
        "bhqk,bqhd->bkhd", grad_scores, query_heads, preferred_element_type=jnp.float32
    ) * (1.0 / HD**0.5)
    row_shape = query_rows.shape
    return (
        grad_query.reshape(row_shape),
        grad_key.reshape(row_shape),
        grad_value.reshape(row_shape),
    )


def local(
    tokens,
    region_mask,
    cotangent,
    cross_qkv,
    cross_q_bias,
    cross_v_bias,
    cross_out,
    cross_out_bias,
    cross_gain,
    cross_shift,
    self_qkv,
    self_q_bias,
    self_v_bias,
    self_out,
    self_out_bias,
    self_gain,
    self_shift,
    ffn_in,
    ffn_in_bias,
    ffn_out,
    ffn_out_bias,
    ffn_gain,
    ffn_shift,
):
    stream_side = lax.axis_index("stream")
    word_mask = jnp.broadcast_to((jnp.arange(LR) < LW).astype(jnp.int32), region_mask.shape)
    own_mask = jnp.where(stream_side == 0, word_mask, region_mask)
    other_mask = jnp.where(stream_side == 0, region_mask, word_mask)
    tok_low = tokens[0].reshape(-1, D)
    tok_rows = tok_low.astype(jnp.float32)
    row_valid = own_mask.reshape(-1, 1).astype(jnp.float32)
    query_rows, key_rows, value_rows = project(tok_low, cross_qkv, cross_q_bias, cross_v_bias)
    far_pair = partner(jnp.concatenate([key_rows, value_rows], axis=1), "stream", 0)
    cross_att, cross_log = attend_forward(query_rows, far_pair[:, :D], far_pair[:, D:], other_mask)
    cross_sum = (
        tok_rows
        + jnp.dot(cross_att, cross_out, preferred_element_type=jnp.float32)
        + cross_out_bias
    )
    joined = layer_norm(cross_sum, cross_gain, cross_shift)
    joined_low = joined.astype(jnp.bfloat16)
    self_query, self_key, self_value = project(
        joined_low, self_qkv[0], self_q_bias[0], self_v_bias[0]
    )
    self_att, self_log = attend_forward(self_query, self_key, self_value, own_mask)
    self_sum = (
        joined
        + jnp.dot(self_att, self_out[0], preferred_element_type=jnp.float32)
        + self_out_bias[0]
    )
    settled = layer_norm(self_sum, self_gain[0], self_shift[0])
    settled_low = settled.astype(jnp.bfloat16)
    ffn_inner = jnp.dot(settled_low, ffn_in[0], preferred_element_type=jnp.float32) + ffn_in_bias[0]
    active, gelu_pull = jax.vjp(partial(jax.nn.gelu, approximate=False), ffn_inner)
    active_low = active.astype(jnp.bfloat16)
    ffn_sum = (
        settled
        + jnp.dot(active_low, ffn_out[0], preferred_element_type=jnp.float32)
        + ffn_out_bias[0]
    )
    normed = layer_norm(ffn_sum, ffn_gain[0], ffn_shift[0]) * row_valid
    stream_out = normed.astype(jnp.bfloat16).reshape(tokens.shape)
    grad_normed = cotangent[0].reshape(-1, D).astype(jnp.float32) * row_valid
    grad_ffn_sum, g_fgain, g_fshift = norm_back(ffn_sum, ffn_gain[0], ffn_shift[0], grad_normed)
    grad_active, g_fout, g_foutb = linear_back(
        active_low, ffn_out[0], grad_ffn_sum.astype(jnp.bfloat16)
    )
    grad_inner = gelu_pull(grad_active)[0].astype(jnp.bfloat16)
    grad_settled, g_fin, g_finb = linear_back(settled_low, ffn_in[0], grad_inner)
    grad_settled = grad_settled + grad_ffn_sum
    grad_self_sum, g_sgain, g_sshift = norm_back(
        self_sum, self_gain[0], self_shift[0], grad_settled
    )
    grad_self_att, g_sout, g_soutb = linear_back(
        self_att, self_out[0], grad_self_sum.astype(jnp.bfloat16)
    )
    grad_query, grad_key, grad_value = attend_back(
        self_query, self_key, self_value, own_mask, self_log, grad_self_att.astype(jnp.bfloat16)
    )
    grad_joined, g_sqkv, g_sqb, g_svb = project_back(
        joined_low,
        self_qkv[0],
        grad_query.astype(jnp.bfloat16),
        grad_key.astype(jnp.bfloat16),
        grad_value.astype(jnp.bfloat16),
    )
    grad_joined = grad_joined + grad_self_sum
    grad_cross_sum, g_cgain, g_cshift = norm_back(cross_sum, cross_gain, cross_shift, grad_joined)
    grad_cross_att, g_cout, g_coutb = linear_back(
        cross_att, cross_out, grad_cross_sum.astype(jnp.bfloat16)
    )
    grad_query, grad_far_key, grad_far_value = attend_back(
        query_rows,
        far_pair[:, :D],
        far_pair[:, D:],
        other_mask,
        cross_log,
        grad_cross_att.astype(jnp.bfloat16),
    )
    returned = partner(
        jnp.concatenate(
            [grad_far_key.astype(jnp.bfloat16), grad_far_value.astype(jnp.bfloat16)], axis=1
        ),
        "stream",
        0,
    )
    grad_tok, g_cqkv, g_cqb, g_cvb = project_back(
        tok_low, cross_qkv, grad_query.astype(jnp.bfloat16), returned[:, :D], returned[:, D:]
    )
    tokens_grad = (grad_tok + grad_cross_sum).reshape(tokens.shape)
    cross_terms = (g_cqkv, g_cqb, g_cvb, g_cout, g_coutb, g_cgain, g_cshift)
    cross_terms = (
        lax.psum(g_cqkv.astype(jnp.bfloat16), "stream").astype(jnp.float32),
        lax.psum(g_cqb.astype(jnp.bfloat16), "stream").astype(jnp.float32),
        lax.psum(g_cvb.astype(jnp.bfloat16), "stream").astype(jnp.float32),
        lax.psum(g_cout.astype(jnp.bfloat16), "stream").astype(jnp.float32),
        lax.psum(g_coutb.astype(jnp.bfloat16), "stream").astype(jnp.float32),
        lax.psum(g_cgain.astype(jnp.bfloat16), "stream").astype(jnp.float32),
        lax.psum(g_cshift.astype(jnp.bfloat16), "stream").astype(jnp.float32),
    )
    summed = (
        lax.psum_scatter(g_sqkv, "dp", scatter_dimension=0, tiled=True),
        lax.psum_scatter(g_sqb, "dp", scatter_dimension=0, tiled=True),
        lax.psum_scatter(g_svb, "dp", scatter_dimension=0, tiled=True),
        lax.psum_scatter(g_sout, "dp", scatter_dimension=0, tiled=True),
        lax.psum_scatter(g_soutb, "dp", scatter_dimension=0, tiled=True),
        lax.psum_scatter(g_sgain, "dp", scatter_dimension=0, tiled=True),
        lax.psum_scatter(g_sshift, "dp", scatter_dimension=0, tiled=True),
        lax.psum_scatter(g_fin, "dp", scatter_dimension=0, tiled=True),
        lax.psum_scatter(g_finb, "dp", scatter_dimension=0, tiled=True),
        lax.psum_scatter(g_fout, "dp", scatter_dimension=0, tiled=True),
        lax.psum_scatter(g_foutb, "dp", scatter_dimension=0, tiled=True),
        lax.psum_scatter(g_fgain, "dp", scatter_dimension=0, tiled=True),
        lax.psum_scatter(g_fshift, "dp", scatter_dimension=0, tiled=True),
        lax.psum_scatter(cross_terms[0], "dp", scatter_dimension=0, tiled=True),
        lax.psum_scatter(cross_terms[1], "dp", scatter_dimension=0, tiled=True),
        lax.psum_scatter(cross_terms[2], "dp", scatter_dimension=0, tiled=True),
        lax.psum_scatter(cross_terms[3], "dp", scatter_dimension=0, tiled=True),
        lax.psum_scatter(cross_terms[4], "dp", scatter_dimension=0, tiled=True),
        lax.psum_scatter(cross_terms[5], "dp", scatter_dimension=0, tiled=True),
        lax.psum_scatter(cross_terms[6], "dp", scatter_dimension=0, tiled=True),
    )
    stream_sums = tuple(summed[:13])
    shared_sums = tuple(summed[13:])
    stream_list = [piece[None] for piece in stream_sums]
    return (
        stream_out,
        tokens_grad,
        shared_sums[0],
        shared_sums[1],
        shared_sums[2],
        shared_sums[3],
        shared_sums[4],
        shared_sums[5],
        shared_sums[6],
        stream_list[0],
        stream_list[1],
        stream_list[2],
        stream_list[3],
        stream_list[4],
        stream_list[5],
        stream_list[6],
        stream_list[7],
        stream_list[8],
        stream_list[9],
        stream_list[10],
        stream_list[11],
        stream_list[12],
    )


def solution(mesh):
    placed = (
        P("stream", "dp", None, None),
        P("dp", None),
        P("stream", "dp", None, None),
        P(),
        P(),
        P(),
        P(),
        P(),
        P(),
        P(),
        P("stream", None, None),
        P("stream", None),
        P("stream", None),
        P("stream", None, None),
        P("stream", None),
        P("stream", None),
        P("stream", None),
        P("stream", None, None),
        P("stream", None),
        P("stream", None, None),
        P("stream", None),
        P("stream", None),
        P("stream", None),
    )
    return jax.shard_map(
        local,
        mesh=mesh,
        in_specs=placed,
        out_specs=(
            P("stream", "dp", None, None),
            P("stream", "dp", None, None),
            P("dp", None),
            P("dp"),
            P("dp"),
            P("dp", None),
            P("dp"),
            P("dp"),
            P("dp"),
            P("stream", "dp", None),
            P("stream", "dp"),
            P("stream", "dp"),
            P("stream", "dp", None),
            P("stream", "dp"),
            P("stream", "dp"),
            P("stream", "dp"),
            P("stream", "dp", None),
            P("stream", "dp"),
            P("stream", "dp", None),
            P("stream", "dp"),
            P("stream", "dp"),
            P("stream", "dp"),
        ),
        check_vma=False,
    )
```

profile of v0, /device:TPU:0, one launch (start us, length us, event | category | flops | bytes accessed | tf_op | source)
XLA Modules:
  0.0 924.3 jit_solution(6695754832540213948)
XLA Ops:
  8.1 2.5 copy.105
  12.7 4.5 fusion.93
  20.0 3.0 collective-permute-start
  31.9 2.7 copy.116
  34.7 2.6 reshape.249
  37.3 4.0 reshape.240
  42.5 19.3 %collective-permute-done = bf16[576,1536]{1,0:T(8,128)(2,1)} collective-permute-done((bf16[576,1536]{1,0:T(8,128)(2,1)}, bf16[576,1536]{1,0:T(8,128)(2,1)}, u32[]{:S(2)}, u32[]{:S(2)}) %collective-permute-start) | collective-permute-done | bytes 1769504 | tf_op jit(solution)/shard_map/ppermute | solution.py:22
  61.9 2.8 fusion.86
  64.6 4.0 reshape.239
  68.6 4.0 reshape.241
  72.6 3.9 fusion.87
  82.9 4.3 convert_element_type.239
  87.2 2.8 fusion.88
  90.4 2.4 fusion.17
  95.5 3.9 reshape.242
  99.4 4.0 reshape.244
  103.4 4.0 reshape.243
  107.4 3.9 fusion.89
  117.8 4.1 convert_element_type.246
  121.9 3.4 fusion.90
  125.7 22.0 %multiply_convert_fusion = (bf16[576,3072]{1,0:T(8,128)(2,1)S(1)}, f32[576,3072]{1,0:T(8,128)}, f32[576,3072]{1,0:T(8,128)}) fusion(f32[3072]{0:T(1024)S(1)} %bitcast.119, bf16[1,768,3072]{2,1,0:T(8,128)(2,1)} %param.40, f32[576,768]{1,0:T(8,128)S(1)} %get-tuple-element.147, f32[768]{0:T(1024)S(1)} %reduce.14, f32[768]{0:T(1024)S(1)} %reduce.13, ...), kind=kOutput, calls=%fused_computation.4 | convolution fusion | flops 2836905984 | bytes 24205824 | tf_op jit(solution)/shard_map/dot_general | solution.py:172
  147.7 3.2 fusion.91
  156.3 9.7 %convert_reduce_fusion = (f32[3072]{0:T(1024)}, bf16[576,3072]{1,0:T(8,128)(2,1)S(1)}) fusion(f32[576,3072]{1,0:T(8,128)} %get-tuple-element.130, bf16[576,768]{1,0:T(8,128)(2,1)S(1)} %get-tuple-element.118, bf16[1,3072,768]{2,1,0:T(8,128)(2,1)S(1)} %bitcast.112, f32[576,3072]{1,0:T(8,128)} %get-tuple-element.148, f32[3072]{0:T(1024)S(1)} %bitcast.120), kind=kOutput, calls=%fused_computation.2 | convolution fusion | flops 2747986944 | bytes 23322624 | tf_op jit(solution)/shard_map/ne,de->nd/dot_general | solution.py:45
  166.1 4.0 multiply_reduce_fusion.4
  175.7 4.0 reshape.246
  179.7 5.5 multiply_reduce_fusion.1
  185.2 3.1 convert_reduce_fusion.1
  189.9 2.4 fusion.42
  196.2 4.2 convert_element_type.261
  200.5 3.5 copy.123
  203.9 4.1 convert_element_type.264
  208.1 3.5 copy.125
  211.6 4.1 convert_element_type.268
  219.6 3.2 multiply_reduce_fusion.5
  228.3 3.9 reshape.247
  232.2 5.5 multiply_reduce_fusion
  237.8 2.5 convert_bitcast_fusion
  245.2 4.3 convert_element_type.277
  249.5 3.5 copy.134
  253.0 4.1 convert_element_type.281
  257.1 3.0 pad_maximum_fusion.1
  261.8 3.6 fusion.92
  267.4 4.1 convert_element_type.274
  272.7 3.6 convolution_convert_fusion.1
  276.3 23.9 %collective-permute-done.1 = bf16[576,1536]{1,0:T(8,128)(2,1)} collective-permute-done((bf16[576,1536]{1,0:T(8,128)(2,1)}, bf16[576,1536]{1,0:T(8,128)(2,1)}, u32[]{:S(2)}, u32[]{:S(2)}) %collective-permute-start.1) | collective-permute-done | bytes 1769504 | tf_op jit(solution)/shard_map/ppermute | solution.py:22
  303.3 4.4 fusion.14
  307.8 3.9 fusion.94
  311.8 116.9 %all-reduce.19.cloned.1.call-done = (bf16[768,2304]{0,1:T(8,128)(2,1)}, bf16[768,768]{1,0:T(8,128)(2,1)}) async-done(((bf16[768,2304]{0,1:T(8,128)(2,1)}, bf16[768,768]{1,0:T(8,128)(2,1)}), (bf16[768,2304]{0,1:T(8,128)(2,1)}, bf16[768,768]{1,0:T(8,128)(2,1)})) %all-reduce.19.cloned.1.call-update) | async-done | bytes 4718608 | tf_op jit(solution)/shard_map/psum | solution.py:232
  428.7 2.9 convert_element_type.288
  431.6 8.4 fusion.78
  440.3 10.4 %fusion.75 = f32[768,3072]{1,0:T(8,128)} fusion(bf16[576,3072]{1,0:T(8,128)(2,1)} %copy-done.20, f32[576,768]{1,0:T(8,128)} %copy-done.7, f32[768]{0:T(1024)S(1)} %reduce.14, f32[768]{0:T(1024)S(1)} %reduce.13, f32[576]{0:T(1024)S(1)} %fusion.73, f32[576]{0:T(1024)S(1)} %broadcast_multiply_fusion.1), kind=kOutput, calls=%fused_computation.165 | convolution fusion | flops 2720120832 | bytes 14756352 | tf_op jit(solution)/shard_map/nd,ne->de/dot_general | solution.py:46
  450.9 9.8 %fusion.95 = f32[3072,768]{1,0:T(8,128)} fusion(bf16[576,3072]{1,0:T(8,128)(2,1)} %copy-done.66, bf16[576,768]{1,0:T(8,128)(2,1)} %copy-done.26), kind=kOutput, calls=%fused_computation.180 | convolution fusion | flops 2717908992 | bytes 13860864 | tf_op jit(solution)/shard_map/nd,ne->de/dot_general | solution.py:46
  460.7 6.1 copy.143
  472.7 2.2 reshape.245
  474.9 2.3 copy.136
  481.2 8.3 all-reduce.15
  489.5 61.3 %all-reduce.14 = (f32[768]{0:T(1024)}, f32[768]{0:T(1024)}, f32[768]{0:T(1024)}, f32[768]{0:T(1024)}, f32[768]{0:T(1024)}, /*index=5*/f32[768]{0:T(1024)}, f32[7...) all-reduce(bf16[768]{0:T(1024)(128)(2,1)} %get-tuple-element.110, ...), channel_id=3, replica_groups=mesh['stream'=2,'dp'=16] {'dp'}, use_global_device_ids=true, to_apply=%region_22.23.clone | all-reduce | flops 13056 | bytes 96768
  557.2 6.9 add_add_fusion.6
  564.0 2.7 reshape.248
  566.7 3.3 copy.137
  576.4 12.4 %reduce-scatter.11.cloned.1.call-done = f32[48,2304]{1,0:T(8,128)} async-done(((f32[768,2304]{1,0:T(8,128)}), f32[48,2304]{1,0:T(8,128)}) %reduce-scatter.11.cloned.1.call-update) | async-done | bytes 442384 | tf_op jit(solution)/shard_map/reduce_scatter | solution.py:241
  588.8 116.3 %reduce-scatter.15.cloned.1.call-done = f32[48,3072]{1,0:T(8,128)} async-done(((f32[768,3072]{1,0:T(8,128)}), f32[48,3072]{1,0:T(8,128)}) %reduce-scatter.15.cloned.1.call-update) | async-done | bytes 589840 | tf_op jit(solution)/shard_map/reduce_scatter | solution.py:248
  705.1 117.0 %reduce-scatter.17.cloned.1.call-done = f32[192,768]{1,0:T(8,128)} async-done(((f32[3072,768]{1,0:T(8,128)}), f32[192,768]{1,0:T(8,128)}) %reduce-scatter.17.cloned.1.call-update) | async-done | bytes 589840 | tf_op jit(solution)/shard_map/reduce_scatter | solution.py:250
  822.1 94.2 %reduce-scatter.19.cloned.1.call-done = f32[48,2304]{1,0:T(8,128)} async-done(((f32[768,2304]{1,0:T(8,128)}), f32[48,2304]{1,0:T(8,128)}) %reduce-scatter.19.cloned.1.call-update) | async-done | bytes 442384
  (240 shorter events, 92.0 us)
Async XLA Ops:
  8.0 82.4 %copy-start = (bf16[1,768,2304]{2,1,0:T(8,128)(2,1)S(1)}, bf16[1,768,2304]{2,1,0:T(8,128)(2,1)}, u32[]{:S(2)}) copy-start(bf16[1,768,2304]{2,1,0:T(8,128)(2,1)} %param.33) | copy-start | bytes 10616836
  8.0 420.6 %all-reduce.19.cloned.1.call-start = ((), (), s32[]{:S(2)}) async-start(), calls=%async_computation.12 | async-start | bytes 9437184 | tf_op jit(solution)/shard_map/psum | solution.py:232
  12.7 4.6 copy-start.54
  12.7 4.6 copy-start.55
  18.6 4.3 copy-start.56
  18.6 4.3 copy-start.57
  20.0 41.9 %collective-permute-start = (bf16[576,1536]{1,0:T(8,128)(2,1)}, bf16[576,1536]{1,0:T(8,128)(2,1)}, u32[]{:S(2)}, u32[]{:S(2)}) collective-permute-start(bf16[576,1536]{1,0:T(8,128)(2,1)} %pad_maximum_fusion), channel_id=1, source_target_pairs={{0,16},{16,0},{1,17},{17,1},{2,18},{18,2},{3,19},{19,3},{4,20},{20... | collective-permute-start | bytes 5308424 | tf_op jit(solution)/shard_map/ppermute | solution.py:22
  31.3 6.0 copy-start.30
  37.3 4.0 copy-start.39
  68.6 4.0 copy-start.59
  76.5 4.5 copy-start.1
  76.5 3.1 copy-start.10
  82.9 4.3 copy-start.64
  87.2 3.2 copy-start.51
  87.2 3.2 copy-start.65
  90.0 2.8 copy-start.15
  90.0 31.9 %copy-start.32 = (f32[576]{0:T(1024)}, f32[576]{0:T(1024)S(1)}, u32[]{:S(2)}) copy-start(f32[576]{0:T(1024)S(1)} %broadcast_multiply_fusion.2) | copy-start | bytes 6916
  90.4 3.5 copy-start.49
  90.4 3.5 copy-start.50
  103.4 4.0 copy-start.58
  111.3 4.5 copy-start.3
  111.3 3.1 copy-start.12
  117.8 4.1 copy-start.43
  121.9 3.8 copy-start.63
  121.9 25.7 %slice-start = ((s8[4718592]{0:T(1024)(128)(4,1)}), s8[4194304]{0:T(1024)(128)(4,1)S(1)}, s32[]{:S(2)}) async-start(s8[4718592]{0:T(1024)(128)(4,1)} %bitcast.111), calls=%async_computation.13 | async-start | bytes 8388608
  125.3 44.8 %copy-start.7 = (f32[576,768]{1,0:T(8,128)}, f32[576,768]{1,0:T(8,128)S(1)}, u32[]{:S(2)}) copy-start(f32[576,768]{1,0:T(8,128)S(1)} %get-tuple-element.147) | copy-start | bytes 5308420
  125.6 22.0 %copy-start.53 = (f32[768]{0:T(1024)S(1)}, f32[768]{0:T(1024)}, u32[]{:S(2)}) copy-start(f32[768]{0:T(1024)} %reduce.15) | copy-start | bytes 9220
  125.7 22.0 %slice-start.1 = ((s8[4718592]{0:T(1024)(128)(4,1)}), s8[524288]{0:T(1024)(128)(4,1)S(1)}, s32[]{:S(2)}) async-start(s8[4718592]{0:T(1024)(128)(4,1)} %bitcast.111), calls=%async_computation.14 | async-start | bytes 1048576
  147.6 3.2 copy-start.66
  147.7 3.6 copy-start.36
  147.7 3.6 copy-start.37
  150.9 2.7 copy-start.48
  153.6 12.4 %slice-start.2 = ((s8[4718592]{0:T(1024)(128)(4,1)}), s8[4194304]{0:T(1024)(128)(4,1)S(1)}, s32[]{:S(2)}) async-start(s8[4718592]{0:T(1024)(128)(4,1)} %bitcast.113), calls=%async_computation.15 | async-start | bytes 8388608
  156.3 9.7 %copy-start.26 = (bf16[576,768]{1,0:T(8,128)(2,1)}, bf16[576,768]{1,0:T(8,128)(2,1)S(1)}, u32[]{:S(2)}) copy-start(bf16[576,768]{1,0:T(8,128)(2,1)S(1)} %get-tuple-element.118) | copy-start | bytes 2654212
  156.3 9.8 %slice-start.3 = ((s8[4718592]{0:T(1024)(128)(4,1)}), s8[524288]{0:T(1024)(128)(4,1)S(1)}, s32[]{:S(2)}) async-start(s8[4718592]{0:T(1024)(128)(4,1)} %bitcast.113), calls=%async_computation.16 | async-start | bytes 1048576
  166.0 4.0 copy-start.20
  170.8 3.0 copy-start.61
  179.6 5.5 copy-start.4
  179.6 5.5 copy-start.5
  179.6 5.5 copy-start.23
  215.6 3.9 copy-start.16
  215.6 3.9 copy-start.19
  215.6 3.9 copy-start.33
  215.6 3.9 copy-start.44
  215.6 3.9 copy-start.47
  215.7 3.9 copy-start.52
  219.6 3.2 copy-start.29
  219.6 3.2 copy-start.35
  223.5 2.9 copy-start.62
  232.2 5.5 copy-start.2
  232.2 5.5 copy-start.6
  232.2 5.5 copy-start.22
  257.1 4.7 copy-start.14
  260.1 40.1 %collective-permute-start.1 = (bf16[576,1536]{1,0:T(8,128)(2,1)}, bf16[576,1536]{1,0:T(8,128)(2,1)}, u32[]{:S(2)}, u32[]{:S(2)}) collective-permute-start(bf16[576,1536]{1,0:T(8,128)(2,1)} %pad_maximum_fusion.1), channel_id=1, source_target_pairs={{0,16},{16,0},{1,17},{17,1},{2,18},{18,2},{3,19},{19,3},{4,20},{20... | collective-permute-start | bytes 5308424 | tf_op jit(solution)/shard_map/ppermute | solution.py:22
  276.3 27.0 %copy-start.24 = (bf16[576,768]{1,0:T(8,128)(2,1)S(1)}, bf16[576,768]{1,0:T(8,128)(2,1)}, u32[]{:S(2)}) copy-start(bf16[576,768]{1,0:T(8,128)(2,1)} %reshape_squeeze.4) | copy-start | bytes 2654212
  307.8 268.7 %reduce-scatter.13.cloned.1.call-start = ((), (), s32[]{:S(2)}) async-start(), calls=%async_computation.8 | async-start | bytes 2506752 | tf_op jit(solution)/shard_map/reduce_scatter | solution.py:244
  311.7 264.7 %reduce-scatter.9.cloned.1.call-start = ((), (), s32[]{:S(2)}) async-start(), calls=%async_computation.6 | async-start | bytes 2506752 | tf_op jit(solution)/shard_map/reduce_scatter | solution.py:257
  431.6 157.3 %reduce-scatter.11.cloned.1.call-start = ((), (), s32[]{:S(2)}) async-start(), calls=%async_computation.7 | async-start | bytes 7520256 | tf_op jit(solution)/shard_map/reduce_scatter | solution.py:241
  440.0 265.1 %reduce-scatter.15.cloned.1.call-start = ((), (), s32[]{:S(2)}) async-start(), calls=%async_computation.9 | async-start | bytes 10027008 | tf_op jit(solution)/shard_map/reduce_scatter | solution.py:248
  450.8 371.3 %reduce-scatter.17.cloned.1.call-start = ((), (), s32[]{:S(2)}) async-start(), calls=%async_computation.10 | async-start | bytes 10027008 | tf_op jit(solution)/shard_map/reduce_scatter | solution.py:250
  460.7 455.7 %reduce-scatter.19.cloned.1.call-start = ((), (), s32[]{:S(2)}) async-start(), calls=%async_computation.11 | async-start | bytes 7520256
  466.8 10.4 %copy-start.38 = (f32[12,64]{1,0:T(8,128)S(1)}, f32[12,64]{1,0:T(8,128)}, u32[]{:S(2)}) copy-start(f32[12,64]{1,0:T(8,128)} %get-tuple-element.161) | copy-start | bytes 9220
  472.7 16.8 %copy-start.40 = (f32[768]{0:T(1024)S(1)}, f32[768]{0:T(1024)}, u32[]{:S(2)}) copy-start(f32[768]{0:T(1024)} %get-tuple-element.88) | copy-start | bytes 9220
  472.7 16.8 %copy-start.41 = (f32[768]{0:T(1024)S(1)}, f32[768]{0:T(1024)}, u32[]{:S(2)}) copy-start(f32[768]{0:T(1024)} %get-tuple-element.117) | copy-start | bytes 9220
  (16 other events, 24.5 us)
Sparse Core Ops, SparseCore 0:
  307.9 120.7 all-reduce.18
Sparse Core Ops, SparseCore 1:
  312.6 64.0 reduce-scatter.12
  431.6 62.8 reduce-scatter.8
  499.5 89.2 reduce-scatter.10
  593.5 111.5 reduce-scatter.14
  710.4 111.7 reduce-scatter.16
  826.8 89.5 reduce-scatter.18
where the time goes:
time: 935 us; the launch traced here: 924 us
  waiting for transfers between devices  500 us (53%)
  local copies, waits for them, and re-layouts  152 us (16%)
  matrix products  143 us (15%)
  blocking collectives  69.6 us (7%)
  other arithmetic  36.2 us (4%)
  between operations  18.2 us (2%)
    reduce_scatter x1, waiting for transfers between devices, local(): lax.psum_scatter(g_fout, 'dp', scatter_dimension=0, tiled=True)  117 us
    psum x1, waiting for transfers between devices, local(): lax.psum(g_cqkv.astype(jnp.bfloat16), 'stream').astype(jnp.float32)  117 us
    reduce_scatter x1, waiting for transfers between devices, local(): lax.psum_scatter(g_fin, 'dp', scatter_dimension=0, tiled=True)  116 us
    unnamed x8, waiting for transfers between devices  94.3 us
    unnamed x1, blocking collectives  61.3 us
    ppermute x2, waiting for transfers between devices, partner(): return lax.ppermute(block, axis, route)  43.2 us
    unnamed x156, local copies, waits for them, and re-layouts  39.1 us
    reshape x8, local copies, waits for them, and re-layouts, split_heads(): return row_block.reshape(row_block.shape[0] // LR, LR, H, HD)  31.7 us
  transfers between devices with their start and end apart: 9, of which 7 were waited for; matrix products, arithmetic and copies ran while one was open for 12% of the time, Pallas kernels for 0%

commit v1 on v0

v1 whole, which is shorter than its diff:
```python
from functools import partial

import jax
import jax.numpy as jnp
from jax import lax
from jax.experimental import pallas as pl
from jax.experimental.pallas import tpu as pltpu
from jax.sharding import PartitionSpec as P

D = 768
H = 12
HD = 64
FF = 3072
LW = 20
LR = 36
BF = jnp.bfloat16
F32 = jnp.float32
GROUP = 4
GR = GROUP * LR
TILE = 256
BLK = 48
FGAIN, FSHIFT, FOUTB, SGAIN, SSHIFT, SOUTB, SQB, SVB, FINB = 0, 1, 2, 3, 4, 5, 6, 7, 8
CGAIN, CSHIFT, COUTB, CQB, CVB = 12, 13, 14, 15, 16
NV = 24


def nn(a, b):
    return lax.dot_general(a, b, (((1,), (0,)), ((), ())), preferred_element_type=F32)


def nt(a, b):
    return lax.dot_general(a, b, (((1,), (1,)), ((), ())), preferred_element_type=F32)


def tn(a, b):
    return lax.dot_general(a, b, (((0,), (0,)), ((), ())), preferred_element_type=F32)


def tile_at(i, size=TILE):
    return pl.ds(pl.multiple_of(i * size, size), size)


def total(x):
    return jnp.sum(x.astype(F32), axis=0, keepdims=True)


def norm_forward(res, gain, shift, hat, rstd, y_low):
    rows = res.shape[0]

    @pl.loop(0, rows // BLK)
    def _(i):
        at = tile_at(i, BLK)
        r = res[at, :]
        centre = r - jnp.mean(r, axis=-1, keepdims=True)
        rs = lax.rsqrt(jnp.mean(centre * centre, axis=-1, keepdims=True) + 1e-12)
        xh = centre * rs
        y = xh * gain[...] + shift[...]
        hat[at, :] = xh.astype(BF)
        rstd[at, :] = rs
        res[at, :] = y
        y_low[at, :] = y.astype(BF)


def norm_grad(dy, xh, rs, gain):
    dx = dy * gain
    return rs * (
        dx - jnp.mean(dx, axis=-1, keepdims=True) - xh * jnp.mean(dx * xh, axis=-1, keepdims=True)
    )


def norm_backward(res, gain, hat, rstd, g_low, vec, at_gain, at_shift, at_bias):
    rows = res.shape[0]

    @pl.loop(0, rows // BLK)
    def _(i):
        at = tile_at(i, BLK)
        dy = res[at, :]
        xh = hat[at, :].astype(F32)
        g = norm_grad(dy, xh, rstd[at, :], gain[...])
        low = g.astype(BF)
        res[at, :] = g
        g_low[at, :] = low
        vec[at_gain : at_gain + 1, :] += total(dy * xh)
        vec[at_shift : at_shift + 1, :] += total(dy)
        vec[at_bias : at_bias + 1, :] += total(low)


def head_masks():
    lane = lax.broadcasted_iota(jnp.int32, (1, 128), 1)
    first = (lane < HD).astype(BF)
    return first, (1 - first).astype(BF)


def stack_heads(x, masks):
    return jnp.concatenate([x * masks[0], x * masks[1]], axis=0)


def pick_heads(x):
    lane = lax.broadcasted_iota(jnp.int32, (GR, 128), 1)
    return jnp.where(lane < HD, x[:GR], x[GR:])


def probabilities(q2, k, rid, kid):
    s = nt(q2, k) * (1.0 / HD**0.5)
    s = jnp.where(rid == kid, s, -1000000000.0)
    e = jnp.exp(s - jnp.max(s, axis=-1, keepdims=True))
    return e * (1.0 / jnp.sum(e, axis=-1, keepdims=True))


def attention_forward(qr, qo, kr, ko, vr, vo, rid, kids, out):
    groups = out.shape[0] // GR

    @pl.loop(0, groups)
    def _(g):
        rows = pl.ds(pl.multiple_of(g * GR, GR), GR)
        kid = kids[g]
        masks = head_masks()

        for p in range(H // 2):
            def cols(o):
                return pl.ds(o + p * 128, 128)

            q2 = stack_heads(qr[rows, cols(qo)], masks)
            prob = probabilities(q2, kr[rows, cols(ko)], rid[...], kid)
            o = nn(prob.astype(BF), vr[rows, cols(vo)])
            out[rows, cols(0)] = pick_heads(o).astype(BF)


def attention_backward(qkv, grad_out, rid, kids):
    groups = grad_out.shape[0] // GR

    @pl.loop(0, groups)
    def _(g):
        rows = pl.ds(pl.multiple_of(g * GR, GR), GR)
        kid = kids[g]
        masks = head_masks()

        for p in range(H // 2):
            def cols(o):
                return pl.ds(o + p * 128, 128)

            q2 = stack_heads(qkv[rows, cols(0)], masks)
            k = qkv[rows, cols(D)]
            v = qkv[rows, cols(2 * D)]
            g2 = stack_heads(grad_out[rows, cols(0)], masks)
            prob = probabilities(q2, k, rid[...], kid)
            gp = nt(g2, v)
            gv = tn(prob.astype(BF), g2)
            s = prob * (gp - jnp.sum(gp * prob, axis=-1, keepdims=True))
            s = s.astype(BF)
            gq = pick_heads(nn(s, k)) * (1.0 / HD**0.5)
            gk = tn(s, q2) * (1.0 / HD**0.5)
            qkv[rows, cols(0)] = gq.astype(BF)
            qkv[rows, cols(D)] = gk.astype(BF)
            qkv[rows, cols(2 * D)] = gv.astype(BF)


SMALL = (
    "cross_q_bias", "cross_v_bias", "cross_out_bias", "cross_gain", "cross_shift",
    "self_q_bias", "self_v_bias", "self_out_bias", "self_gain", "self_shift",
    "ffn_in_bias", "ffn_out_bias", "ffn_gain", "ffn_shift",
)
NS = len(SMALL)
PARTS = (
    [(4 * BLK, TILE)] * 3 + [(BLK, 1024)] * 3 + [(BLK, D)] * 8
)


def body(*refs):
    tok_h, far_h, cot_h, cqkv_h, cout_h, sqkv_h, sout_h, fin_h, fout_h = refs[:9]
    kid_own, kid_far, row_ok = refs[9:12]
    sm = dict(zip(SMALL, refs[12 : 12 + NS]))
    refs = refs[12 + NS :]
    out_o, grad_o, back_o, vec = refs[:4]
    parts_o = refs[4 : 4 + len(PARTS)]
    refs = refs[4 + len(PARTS) :]
    (tok, far, cot, wp, wq, xqkv, xatt, joined, hat1, sqkv, satt, settled, hat2, active, inner,
     res, g_low, g_att, rid, rstd1, rstd2, slot_a, slot_b, sems, part_sems) = refs
    rows = tok.shape[0]

    def fetch(i, src, dst):
        c = pltpu.make_async_copy(src, dst, sems.at[i])
        c.start()
        return c

    c_tok = fetch(0, tok_h, tok)
    c_cqkv = fetch(1, cqkv_h, wp.at[:, 0 : 3 * D])
    c_far = fetch(2, far_h, far)
    c_cout = fetch(3, cout_h, wp.at[:, 3 * D :])
    c_sqkv = [fetch(4 + j, sqkv_h.at[:, j * D : (j + 1) * D], wq.at[j * D : (j + 1) * D, :]) for j in range(3)]
    c_sout = fetch(7, sout_h, wq.at[3 * D :, :])
    c_cot = fetch(8, cot_h, cot)

    vec[...] = jnp.zeros_like(vec)
    row_item = lax.broadcasted_iota(jnp.int32, (2 * GR, GR), 0)
    item = jnp.zeros((2 * GR, GR), F32)
    for edge in range(1, 2 * GROUP):
        if edge == GROUP:
            continue
        item += (row_item >= edge * LR).astype(F32)
    item -= jnp.where(row_item >= GR, float(GROUP - 1), 0.0)
    rid[...] = item

    c_tok.wait()
    c_cqkv.wait()

    @pl.loop(0, 3)
    def _(j):
        at = tile_at(j)
        xqkv[:, at] = (nn(tok[...], wp[:, at]) + sm["cross_q_bias"][:, at]).astype(BF)

    c_far.wait()

    @pl.loop(3, 6)
    def _(j):
        at = tile_at(j)
        xqkv[:, at] = nn(far[...], wp[:, at]).astype(BF)

    @pl.loop(6, 9)
    def _(j):
        at = tile_at(j)
        xqkv[:, at] = (nn(far[...], wp[:, at]) + sm["cross_v_bias"][:, tile_at(j - 6)]).astype(BF)

    attention_forward(xqkv, 0, xqkv, D, xqkv, 2 * D, rid, kid_far, xatt)
    c_cout.wait()

    @pl.loop(0, 3)
    def _(j):
        at = tile_at(j)
        w_at = pl.ds(pl.multiple_of(3 * D + j * TILE, TILE), TILE)
        res[:, at] = tok[:, at].astype(F32) + nn(xatt[...], wp[:, w_at]) + sm["cross_out_bias"][:, at]

    c_fin = fetch(1, fin_h, wp)
    norm_forward(res, sm["cross_gain"], sm["cross_shift"], hat1, rstd1, joined)

    for c in c_sqkv:
        c.wait()
    for part in range(3):
        @pl.loop(0, 3)
        def _(j):
            at = tile_at(j)
            x = nn(joined[...], wq[part * D : (part + 1) * D, at])
            if part == 0:
                x = x + sm["self_q_bias"][:, at]
            if part == 2:
                x = x + sm["self_v_bias"][:, at]
            sqkv[:, pl.ds(pl.multiple_of(part * D + j * TILE, TILE), TILE)] = x.astype(BF)

    attention_forward(sqkv, 0, sqkv, D, sqkv, 2 * D, rid, kid_own, satt)
    c_sout.wait()

    @pl.loop(0, 3)
    def _(j):
        at = tile_at(j)
        res[:, at] += nn(satt[...], wq[3 * D :, at]) + sm["self_out_bias"][:, at]

    c_fout = fetch(3, fout_h, wq)
    norm_forward(res, sm["self_gain"], sm["self_shift"], hat2, rstd2, settled)

    c_fin.wait()

    @pl.loop(0, FF // TILE)
    def _(j):
        at = tile_at(j)
        x = nn(settled[...], wp[:, at]) + sm["ffn_in_bias"][:, at]
        half = 0.5 * (1.0 + lax.erf(x * (0.5**0.5)))
        active[:, at] = (x * half).astype(BF)
        inner[:, at] = (half + x * jnp.exp(-0.5 * x * x) * 0.3989422804014327).astype(BF)

    c_fout.wait()

    @pl.loop(0, 3)
    def _(j):
        at = tile_at(j)
        res[:, at] += nn(active[...], wq[:, at]) + sm["ffn_out_bias"][:, at]

    c_cot.wait()

    @pl.loop(0, rows // BLK)
    def _(i):
        at = tile_at(i, BLK)
        r = res[at, :]
        ok = row_ok[at, :]
        gain = sm["ffn_gain"][...]
        centre = r - jnp.mean(r, axis=-1, keepdims=True)
        rs = lax.rsqrt(jnp.mean(centre * centre, axis=-1, keepdims=True) + 1e-12)
        xh = centre * rs
        y = xh * gain + sm["ffn_shift"][...]
        g_low[at, :] = (y * ok).astype(BF)
        dy = cot[at, :].astype(F32) * ok
        g = norm_grad(dy, xh, rs, gain)
        low = g.astype(BF)
        res[at, :] = g
        cot[at, :] = low
        vec[FGAIN : FGAIN + 1, :] += total(dy * xh)
        vec[FSHIFT : FSHIFT + 1, :] += total(dy)
        vec[FOUTB : FOUTB + 1, :] += total(low)

    c_out = fetch(8, g_low, out_o)

    used = {0: [], 1: []}

    def slot_for(i):
        kind = 1 if PARTS[i][0] != BLK else 0
        held = used[kind]
        if len(held) >= 2:
            held[-2].wait()
        place = len(held) % 2
        ref = (slot_b if kind else slot_a).at[place]
        if not kind and PARTS[i][1] != 1024:
            ref = ref.at[:, :, :, 0 : PARTS[i][1]]
        return kind, ref

    def push(i, kind, ref):
        c = pltpu.make_async_copy(ref, parts_o[i], part_sems.at[i])
        c.start()
        used[kind].append(c)

    def weight_part(i, left, right, col0, bias=None):
        kind, ref = slot_for(i)
        width = PARTS[i][1]

        @pl.loop(0, width // TILE)
        def _(j):
            src = right[:, pl.ds(pl.multiple_of(col0 + j * TILE, TILE), TILE)]
            w = tn(left[...], src).astype(BF)
            for d in range(16):
                ref[d % 2, d // 2, :, tile_at(j)] = w[d * BLK : (d + 1) * BLK, :]
            if bias is not None:
                vec[bias : bias + 1, tile_at(j)] += total(src)

        push(i, kind, ref)

    for col in range(3):
        kind, ref = slot_for(col)

        @pl.loop(0, 4)
        def _(t):
            w = tn(active[:, tile_at(t, D)], cot[:, col * TILE : (col + 1) * TILE]).astype(BF)
            for d in range(4):
                ref[d % 2, t * 2 + d // 2, :, :] = w[d * 4 * BLK : (d + 1) * 4 * BLK, :]

        push(col, kind, ref)

    @pl.loop(0, FF // TILE)
    def _(j):
        at = tile_at(j)
        ga = nt(cot[...], wq[at, :])
        gi = (ga * inner[:, at].astype(F32)).astype(BF)
        inner[:, at] = gi

    for r in range(4):
        vec[FINB + r : FINB + r + 1, :] = total(inner[:, r * D : (r + 1) * D])

    c_sqkv = [fetch(4 + j, sqkv_h.at[:, j * D : (j + 1) * D], wq.at[j * D : (j + 1) * D, :]) for j in range(3)]
    c_sout = fetch(7, sout_h, wq.at[3 * D :, :])

    for col in range(3):
        weight_part(3 + col, settled, inner, col * 1024)

    @pl.loop(0, 3)
    def _(j):
        at = tile_at(j)
        res[:, at] += nt(inner[...], wp[at, :])

    c_cqkv = fetch(1, cqkv_h, wp.at[:, 0 : 3 * D])
    c_cout = fetch(3, cout_h, wp.at[:, 3 * D :])
    c_out.wait()
    norm_backward(res, sm["self_gain"], hat2, rstd2, g_low, vec, SGAIN, SSHIFT, SOUTB)
    weight_part(6, satt, g_low, 0)
    for c in c_sqkv:
        c.wait()
    c_sout.wait()

    @pl.loop(0, 3)
    def _(j):
        at = tile_at(j)
        w_at = pl.ds(pl.multiple_of(3 * D + j * TILE, TILE), TILE)
        g_att[:, at] = nt(g_low[...], wq[w_at, :]).astype(BF)

    attention_backward(sqkv, g_att, rid, kid_own)
    for part in range(3):
        weight_part(7 + part, joined, sqkv, part * D, (SQB, None, SVB)[part])

    @pl.loop(0, 3)
    def _(j):
        at = tile_at(j)
        g = res[:, at]
        for part in range(3):
            w_at = pl.ds(pl.multiple_of(part * D + j * TILE, TILE), TILE)
            g += nt(sqkv[:, part * D : (part + 1) * D], wq[w_at, :])
        res[:, at] = g

    norm_backward(res, sm["cross_gain"], hat1, rstd1, g_low, vec, CGAIN, CSHIFT, COUTB)
    weight_part(10, xatt, g_low, 0)
    c_cqkv.wait()
    c_cout.wait()

    @pl.loop(0, 3)
    def _(j):
        at = tile_at(j)
        g_att[:, at] = nt(g_low[...], wp[at, 3 * D :]).astype(BF)

    attention_backward(xqkv, g_att, rid, kid_far)

    @pl.loop(0, 3)
    def _(j):
        at = tile_at(j)
        g_att[:, at] = nt(xqkv[:, D:], wp[at, D : 3 * D]).astype(BF)
        res[:, at] += nt(xqkv[:, 0:D], wp[at, 0:D])

    c_back = fetch(8, g_att, back_o)
    c_grad = fetch(0, res, grad_o)
    weight_part(11, tok, xqkv, 0, CQB)
    weight_part(12, far, xqkv, D)
    weight_part(13, far, xqkv, 2 * D, CVB)
    for held in used.values():
        for c in held[-2:]:
            c.wait()
    c_back.wait()
    c_grad.wait()


def compute(rows, arrays):
    any_space = pl.BlockSpec(memory_space=pl.ANY)
    vmem = pl.BlockSpec(memory_space=pltpu.VMEM)
    part_shapes = [jax.ShapeDtypeStruct((2, 8, r, n), BF) for r, n in PARTS]
    low = lambda n=D: pltpu.VMEM((rows, n), BF)
    return pl.pallas_call(
        body,
        out_shape=[
            jax.ShapeDtypeStruct((rows, D), BF),
            jax.ShapeDtypeStruct((rows, D), F32),
            jax.ShapeDtypeStruct((rows, D), BF),
            jax.ShapeDtypeStruct((NV, D), F32),
            *part_shapes,
        ],
        in_specs=[any_space] * 9 + [vmem] * (3 + NS),
        out_specs=[any_space] * 3 + [vmem] + [any_space] * len(PARTS),
        scratch_shapes=[
            low(), low(), low(),
            pltpu.VMEM((D, FF), BF), pltpu.VMEM((FF, D), BF),
            low(3 * D), low(), low(), low(),
            low(3 * D), low(), low(), low(),
            low(FF), low(FF),
            pltpu.VMEM((rows, D), F32), low(), low(),
            pltpu.VMEM((2 * GR, GR), F32),
            pltpu.VMEM((rows, 1), F32), pltpu.VMEM((rows, 1), F32),
            pltpu.VMEM((2, 2, 8, BLK, 1024), BF), pltpu.VMEM((2, 2, 8, 4 * BLK, TILE), BF),
            pltpu.SemaphoreType.DMA((9,)), pltpu.SemaphoreType.DMA((len(PARTS),)),
        ],
        compiler_params=pltpu.CompilerParams(vmem_limit_bytes=62 * 2**20),
    )(*arrays)


NAMES = (
    "tokens", "region_mask", "cotangent", "cross_qkv", "cross_q_bias", "cross_v_bias",
    "cross_out", "cross_out_bias", "cross_gain", "cross_shift", "self_qkv", "self_q_bias",
    "self_v_bias", "self_out", "self_out_bias", "self_gain", "self_shift", "ffn_in",
    "ffn_in_bias", "ffn_out", "ffn_out_bias", "ffn_gain", "ffn_shift",
)


def partner(block):
    return lax.ppermute(block, "stream", [(0, 1), (1, 0)])


def local(*args):
    a = dict(zip(NAMES, args))
    side = lax.axis_index("stream")
    tokens = a["tokens"]
    tok = tokens[0].reshape(-1, D)
    cot = a["cotangent"][0].reshape(-1, D)
    rows = tok.shape[0]
    far = partner(tok)
    mask = a["region_mask"]
    word = jnp.broadcast_to((jnp.arange(LR) < LW).astype(jnp.int32), mask.shape)
    own = jnp.where(side == 0, word, mask)
    other = jnp.where(side == 0, mask, word)
    place = (jnp.arange(rows) // LR) % GROUP

    def key_ids(m):
        return jnp.where(m.reshape(-1) > 0, place, -1).astype(F32).reshape(rows // GR, 1, GR)

    row_ok = own.reshape(-1, 1).astype(F32)
    small = [a[n].reshape(1, -1) for n in SMALL]
    outs = compute(
        rows,
        [tok, far, cot, a["cross_qkv"], a["cross_out"], a["self_qkv"][0], a["self_out"][0],
         a["ffn_in"][0], a["ffn_out"][0], key_ids(own), key_ids(other), row_ok, *small],
    )
    stream_out, grad_tok, back, vec = outs[:4]
    parts = outs[4:]
    tokens_grad = (grad_tok + partner(back).astype(F32)).reshape(tokens.shape)

    def natural(some):
        done = []
        for p in some:
            r, n = p.shape[2:]
            done.append(p.transpose(1, 0, 2, 3).reshape(16 * r, n))
        return jnp.concatenate(done, axis=1)

    def scatter(x, axes=("dp",)):
        if len(axes) > 1:
            x = lax.psum(x, "stream")
        return lax.psum_scatter(x, "dp", scatter_dimension=0, tiled=True).astype(F32)

    fout = scatter(natural(parts[0:3]))
    fin = scatter(natural(parts[3:6]))
    sout = scatter(natural(parts[6:7]))
    sqkv = scatter(natural(parts[7:10]))
    cout = scatter(natural(parts[10:11]), ("stream", "dp"))
    cqkv = scatter(natural(parts[11:14]), ("stream", "dp"))
    own_vec = lax.psum(vec[:12], "dp")
    cross_vec = lax.psum(vec[12:], ("stream", "dp"))
    n = lax.axis_size("dp")
    me = lax.axis_index("dp")

    def mine(v, r):
        return lax.dynamic_slice_in_dim(v[r], me * (D // n), D // n)

    def own_v(r):
        return mine(own_vec, r)[None]

    def cross_v(r):
        return mine(cross_vec, r - 12)

    finb = lax.dynamic_slice_in_dim(own_vec[FINB : FINB + 4].reshape(-1), me * (FF // n), FF // n)[None]
    return (
        stream_out.reshape(tokens.shape), tokens_grad,
        cqkv, cross_v(CQB), cross_v(CVB), cout, cross_v(COUTB), cross_v(CGAIN), cross_v(CSHIFT),
        sqkv[None], own_v(SQB), own_v(SVB), sout[None], own_v(SOUTB), own_v(SGAIN), own_v(SSHIFT),
        fin[None], finb, fout[None], own_v(FOUTB), own_v(FGAIN), own_v(FSHIFT),
    )


def solution(mesh):
    both = P("stream", "dp")
    one = P("stream")
    specs = {n: one for n in NAMES}
    specs.update({n: P() for n in NAMES if n.startswith("cross")})
    specs.update(tokens=both, cotangent=both, region_mask=P("dp"))
    return jax.shard_map(
        local,
        mesh=mesh,
        in_specs=tuple(specs[n] for n in NAMES),
        out_specs=(both, both) + (P("dp"),) * 7 + (both,) * 13,
        check_vma=False,
    )
```

time: 935 us -> 612 us (0.65); the launches traced: 924 us -> 611 us
  waiting for transfers between devices: 500 us -> 315 us
  matrix products: 143 us -> 0 us
  Pallas kernels: 0 us -> 123 us
  local copies, waits for them, and re-layouts: 152 us -> 36.9 us
  blocking collectives: 69.6 us -> 95.6 us
  other arithmetic: 36.2 us -> 22.2 us
    dot_general x30 -> x0, matrix products: 143 us -> none  [the longest x4 27.8 us: linear_back(): jnp.einsum('nd,ne->de', low_rows, grad_low, preferred_element_type=jnp.fl...]
    pallas_call x0 -> x1, Pallas kernels: none -> 123 us  [compute(): pl.pallas_call(body, out_shape=[jax.ShapeDtypeStruct((rows, D), BF), jax....]
    unnamed x8 -> x7, waiting for transfers between devices: 94.3 us -> 0.11 us
    psum x1, waiting for transfers between devices: 117 us -> 23.3 us  [scatter(): x = lax.psum(x, 'stream')]
    psum x1 -> x2, blocking collectives: 8.29 us -> 95.6 us  [the longest x1 57.7 us: local(): own_vec = lax.psum(vec[:12], 'dp')]
    unnamed x1 -> x0, blocking collectives: 61.3 us -> none
    convert_element_type x20 -> x1, local copies, waits for them, and re-layouts: 60 us -> 0.86 us  [local(): row_ok = own.reshape(-1, 1).astype(F32)]
    reduce_scatter x5 -> x6, waiting for transfers between devices: 246 us -> 278 us  [scatter(): lax.psum_scatter(x, 'dp', scatter_dimension=0, tiled=True).astype(F32)]
  transfers between devices with their start and end apart: 9 -> 9, of which waited for: 7 -> 7; matrix products, arithmetic and copies ran while one was open for 12% -> 7% of each run, Pallas kernels for 0% -> 0%
where the time goes in v1:
time: 612 us; the launch traced here: 611 us
  waiting for transfers between devices  315 us (51%)
  Pallas kernels  123 us (20%)
  blocking collectives  95.6 us (16%)
  local copies, waits for them, and re-layouts  36.9 us (6%)
  other arithmetic  22.2 us (4%)
  between operations  14.5 us (2%)
    reduce_scatter x6, waiting for transfers between devices, scatter(): lax.psum_scatter(x, 'dp', scatter_dimension=0, tiled=True).astype(F32)  278 us
    pallas_call x1, Pallas kernels, compute(): pl.pallas_call(body, out_shape=[jax.ShapeDtypeStruct((rows, D), BF), jax....  123 us
    psum x1, blocking collectives, local(): own_vec = lax.psum(vec[:12], 'dp')  57.7 us
    psum x1, blocking collectives, local(): cross_vec = lax.psum(vec[12:], ('stream', 'dp'))  37.8 us
    psum x1, waiting for transfers between devices, scatter(): x = lax.psum(x, 'stream')  23.3 us
    unnamed x50, local copies, waits for them, and re-layouts  14.4 us
    ppermute x2, waiting for transfers between devices, partner(): return lax.ppermute(block, 'stream', [(0, 1), (1, 0)])  13.7 us
  transfers between devices with their start and end apart: 9, of which 7 were waited for; matrix products, arithmetic and copies ran while one was open for 7% of the time, Pallas kernels for 0%

profile of v1, /device:TPU:0, one launch (start us, length us, event | category | flops | bytes accessed | tf_op | source)
XLA Modules:
  0.0 611.4 jit_solution(1550569662274529041)
XLA Ops:
  7.2 1.5 copy.49
  8.9 3.0 collective-permute-start
  12.3 1.1 reshape_squeeze.7.refs_2_
  13.6 0.9 convert_element_type.51.refs_11_
  14.5 0.6 reshape.260.refs_12_
  15.1 0.6 reshape.261.refs_13_
  15.6 0.6 reshape.262.refs_14_
  16.2 0.6 reshape.263.refs_15_
  16.8 0.6 reshape.264.refs_16_
  17.4 0.6 select_convert_fusion.1
  18.1 13.7 %collective-permute-done.refs_1_ = bf16[576,768]{1,0:T(8,128)(2,1)} collective-permute-done((bf16[576,768]{1,0:T(8,128)(2,1)S(1)}, bf16[576,768]{1,0:T(8,128)(2,1)}, u32[]{:S(2)}, u32[]{:S(2)}) %collective-permute-start) | collective-permute-done | bytes 884768 | tf_op jit(solution)/shard_map/ppermute | solution.py:465
  31.7 122.7 %shard_map.390 = (bf16[576,768]{1,0:T(8,128)(2,1)}, f32[576,768]{1,0:T(8,128)}, bf16[576,768]{1,0:T(8,128)(2,1)}, f32[24,768]{1,0:T(8,128)}, bf16[2,8,192,256]{3...) custom-call(bf16[576,768]{1,0:T(8,128)(2,1)} %copy-done, ...), custom_call_target="tpu_custom_call" | custom-call | tf_op jit(solution)/shard_map/pallas_call | solution.py:429
  154.5 2.5 copy.57
  157.1 1.1 copy-done.13
  158.7 1.9 pad_maximum_fusion.2
  160.7 1.2 copy-done.11
  161.9 1.1 copy.61
  163.0 0.5 copy-done.10
  163.7 0.7 copy-done.9
  164.5 0.6 copy-done.8
  165.1 2.3 pad_maximum_fusion.3
  167.4 1.3 copy-done.7
  169.0 0.3 copy-done.6
  169.5 1.0 copy-done.5
  170.5 1.3 copy.62
  171.8 44.9 %reduce-scatter.17.cloned.1.call-done = bf16[48,768]{1,0:T(8,128)(2,1)} async-done(((bf16[768,768]{1,0:T(8,128)(2,1)}), bf16[48,768]{1,0:T(8,128)(2,1)}) %reduce-scatter.17.cloned.1.call-update) | async-done | bytes 73744 | tf_op jit(solution)/shard_map/reduce_scatter | solution.py:506
  216.7 71.0 %reduce-scatter.15.cloned.1.call-done = bf16[48,2304]{1,0:T(8,128)(2,1)} async-done(((bf16[768,2304]{1,0:T(8,128)(2,1)}), bf16[48,2304]{1,0:T(8,128)(2,1)}) %reduce-scatter.15.cloned.1.call-update) | async-done | bytes 221200 | tf_op jit(solution)/shard_map/reduce_scatter | solution.py:506
  287.8 3.4 pad_maximum_fusion
  291.3 1.3 copy-done.4
  292.7 0.4 copy-done.3
  293.2 1.0 copy-done.2
  294.3 2.4 pad_maximum_fusion.1
  296.8 1.4 reshape.265
  298.2 1.1 copy.68
  299.3 1.5 collective-permute-start.1
  300.8 57.7 %psum.31 = f32[12,768]{1,0:T(8,128)S(1)} all-reduce(f32[12,768]{1,0:T(8,128)S(1)} %get-tuple-element.104), channel_id=1, replica_groups=mesh['stream'=2,'dp'=16] {'dp'}, use_global_device_ids=true, to_apply=%region_6.7 | all-reduce | flops 9216 | bytes 73728 | tf_op jit(solution)/shard_map/psum | solution.py:514
  358.5 0.6 dynamic_slice.67
  359.1 37.8 %psum.29 = f32[12,768]{1,0:T(8,128)S(1)} all-reduce(f32[12,768]{1,0:T(8,128)S(1)} %get-tuple-element.105), channel_id=1, replica_groups=mesh['stream'=2,'dp'=16] {'stream','dp'}, use_global_device_ids=true, to_apply=%region_2.3 | all-reduce | flops 9216 | bytes 73728 | tf_op jit(solution)/shard_map/psum | solution.py:515
  397.0 0.6 fusion.1
  397.6 0.6 fusion.2
  398.2 0.6 fusion.3
  398.8 0.6 fusion.4
  399.3 0.6 fusion.5
  399.9 0.6 constant_dynamic-slice_fusion.7
  400.5 0.6 constant_dynamic-slice_fusion.6
  401.1 0.6 constant_dynamic-slice_fusion.5
  401.7 0.6 constant_dynamic-slice_fusion.4
  402.3 0.6 constant_dynamic-slice_fusion.3
  402.9 0.6 constant_dynamic-slice_fusion.2
  403.4 0.6 constant_dynamic-slice_fusion.1
  404.0 0.6 constant_dynamic-slice_fusion
  404.6 1.4 convert_add_fusion
  406.0 1.5 reshape.266
  407.5 1.7 copy.69
  409.3 1.6 bitcast_convert_fusion.3
  410.8 8.6 %reduce-scatter.7.cloned.1.call-done = bf16[48,2304]{1,0:T(8,128)(2,1)} async-done(((bf16[768,2304]{1,0:T(8,128)(2,1)}), bf16[48,2304]{1,0:T(8,128)(2,1)}) %reduce-scatter.7.cloned.1.call-update) | async-done | bytes 221200 | tf_op jit(solution)/shard_map/reduce_scatter | solution.py:506
  419.4 1.7 bitcast_convert_fusion.2
  421.2 23.3 %all-reduce.3.cloned.1.call-done = (bf16[48,2304]{1,0:T(8,128)(2,1)}, bf16[48,768]{1,0:T(8,128)(2,1)}) async-done(((bf16[48,2304]{1,0:T(8,128)(2,1)}, bf16[48,768]{1,0:T(8,128)(2,1)}), (bf16[48,2304]{1,0:T(8,128)(2,1)}, bf16[48,768]{1,0:T(8,128)(2,1)})) %all-reduce.3.cloned.1.call-update) | async-done | bytes 294928 | tf_op jit(solution)/shard_map/psum | solution.py:505
  444.5 1.7 convert_element_type.49
  446.2 1.6 convert_element_type.50
  447.7 76.0 %reduce-scatter.11.cloned.1.call-done = bf16[48,3072]{1,0:T(8,128)(2,1)} async-done(((bf16[768,3072]{1,0:T(8,128)(2,1)}), bf16[48,3072]{1,0:T(8,128)(2,1)}) %reduce-scatter.11.cloned.1.call-update) | async-done | bytes 294928 | tf_op jit(solution)/shard_map/reduce_scatter | solution.py:506
  523.8 1.8 bitcast_convert_fusion.1
  525.6 77.1 %reduce-scatter.13.cloned.1.call-done = bf16[192,768]{1,0:T(8,128)(2,1)} async-done(((bf16[3072,768]{1,0:T(8,128)(2,1)}), bf16[192,768]{1,0:T(8,128)(2,1)}) %reduce-scatter.13.cloned.1.call-update) | async-done | bytes 294928 | tf_op jit(solution)/shard_map/reduce_scatter | solution.py:506
  602.7 1.8 bitcast_convert_fusion
  (74 shorter events, 2.6 us)
Async XLA Ops:
  7.2 4.8 copy-start.15
  7.2 209.5 %reduce-scatter.17.cloned.1.call-start = ((), (), s32[]{:S(2)}) async-start(), calls=%async_computation.11 | async-start | bytes 1253376 | tf_op jit(solution)/shard_map/reduce_scatter | solution.py:506
  8.9 4.5 copy-start
  8.9 22.8 %collective-permute-start = (bf16[576,768]{1,0:T(8,128)(2,1)S(1)}, bf16[576,768]{1,0:T(8,128)(2,1)}, u32[]{:S(2)}, u32[]{:S(2)}) collective-permute-start(bf16[576,768]{1,0:T(8,128)(2,1)S(1)} %reshape_squeeze.6.refs_0_), channel_id=1, source_target_pairs={{0,16},{16,0},{1,17},{17,1},{2,18},{18,2},{3,19},{19,3},{4,20},{20... | collective-permute-start | bytes 2654216 | tf_op jit(solution)/shard_map/ppermute | solution.py:465
  12.0 1.4 copy-start.17
  12.0 2.5 copy-start.18
  12.0 3.1 copy-start.19
  12.0 3.7 copy-start.20
  12.0 4.2 copy-start.21
  12.0 4.8 copy-start.22
  154.5 2.6 copy-start.14
  157.0 1.3 copy-start.13
  157.0 130.7 %reduce-scatter.15.cloned.1.call-start = ((), (), s32[]{:S(2)}) async-start(), calls=%async_computation.10 | async-start | bytes 3760128 | tf_op jit(solution)/shard_map/reduce_scatter | solution.py:506
  157.1 1.5 copy-start.12
  160.6 1.3 copy-start.11
  160.6 248.6 %reduce-scatter.9.cloned.1.call-start = ((), (), s32[]{:S(2)}) async-start(), calls=%async_computation.7 | async-start | bytes 1253376 | tf_op jit(solution)/shard_map/reduce_scatter | solution.py:506
  161.9 1.7 copy-start.10
  163.0 1.4 copy-start.9
  163.0 256.4 %reduce-scatter.7.cloned.1.call-start = ((), (), s32[]{:S(2)}) async-start(), calls=%async_computation.6 | async-start | bytes 3760128 | tf_op jit(solution)/shard_map/reduce_scatter | solution.py:506
  163.7 1.4 copy-start.8
  167.4 1.4 copy-start.7
  167.4 277.1 %all-reduce.3.cloned.1.call-start = ((), (), s32[]{:S(2)}) async-start(), calls=%async_computation.12 | async-start | bytes 589824 | tf_op jit(solution)/shard_map/psum | solution.py:505
  167.4 1.9 copy-start.6
  169.0 1.5 copy-start.5
  287.7 236.1 %reduce-scatter.11.cloned.1.call-start = ((), (), s32[]{:S(2)}) async-start(), calls=%async_computation.8 | async-start | bytes 5013504 | tf_op jit(solution)/shard_map/reduce_scatter | solution.py:506
  291.2 1.4 copy-start.4
  291.2 1.9 copy-start.3
  291.2 311.5 %reduce-scatter.13.cloned.1.call-start = ((), (), s32[]{:S(2)}) async-start(), calls=%async_computation.9 | async-start | bytes 5013504 | tf_op jit(solution)/shard_map/reduce_scatter | solution.py:506
  292.7 1.5 copy-start.2
  296.8 4.0 copy-start.16
  296.8 107.8 %copy-start.1 = (f32[576,768]{1,0:T(8,128)S(1)}, f32[576,768]{1,0:T(8,128)}, u32[]{:S(2)}) copy-start(f32[576,768]{1,0:T(8,128)} %get-tuple-element.41) | copy-start | bytes 5308420
  299.3 105.3 %collective-permute-start.1 = (bf16[576,768]{1,0:T(8,128)(2,1)}, bf16[576,768]{1,0:T(8,128)(2,1)S(1)}, u32[]{:S(2)}, u32[]{:S(2)}) collective-permute-start(bf16[576,768]{1,0:T(8,128)(2,1)} %get-tuple-element.42), channel_id=1, source_target_pairs={{0,16},{16,0},{1,17},{17,1},{2,18},{18,2},{3,19},{19,3},{4,20},{20... | collective-permute-start | bytes 2654216 | tf_op jit(solution)/shard_map/ppermute | solution.py:465
Sparse Core Ops, SparseCore 0:
  157.1 59.5 reduce-scatter.16
  220.5 67.0 reduce-scatter.14
  291.3 57.0 reduce-scatter.8
  352.1 67.2 reduce-scatter.6
  421.7 22.7 all-reduce.2
  448.2 75.5 reduce-scatter.10
  528.1 74.5 reduce-scatter.12

commit v2 on v1

v2 whole, which is shorter than its diff:
```python
from functools import partial
from types import SimpleNamespace

import jax
import jax.numpy as jnp
from jax import lax
from jax.experimental import pallas as pl
from jax.experimental.pallas import tpu as pltpu
from jax.sharding import PartitionSpec as P

D = 768
H = 12
HD = 64
FF = 3072
LW = 20
LR = 36
BF = jnp.bfloat16
F32 = jnp.float32
GROUP = 4
GR = GROUP * LR
PAIR = 2 * LR
PAD = 80
TILE = 256
BLK = 48
FGAIN, FSHIFT, FOUTB, SGAIN, SSHIFT, SOUTB, SQB, SVB, FINB = 0, 1, 2, 3, 4, 5, 6, 7, 8
CGAIN, CSHIFT, COUTB, CQB, CVB = 12, 13, 14, 15, 16
NV = 24


def nn(a, b):
    return lax.dot_general(a, b, (((1,), (0,)), ((), ())), preferred_element_type=F32)


def nt(a, b):
    return lax.dot_general(a, b, (((1,), (1,)), ((), ())), preferred_element_type=F32)


def tn(a, b):
    return lax.dot_general(a, b, (((0,), (0,)), ((), ())), preferred_element_type=F32)


def tile_at(i, size=TILE):
    return pl.ds(pl.multiple_of(i * size, size), size)


def total(x):
    return jnp.sum(x.astype(F32), axis=0, keepdims=True)


def norm_forward(res, gain, shift, hat, columns, col, y_low):
    rows = res.shape[0]

    @pl.loop(0, rows // BLK)
    def _(i):
        at = tile_at(i, BLK)
        r = res[at, :]
        centre = r - jnp.mean(r, axis=-1, keepdims=True)
        rs = lax.rsqrt(jnp.mean(centre * centre, axis=-1, keepdims=True) + 1e-12)
        xh = centre * rs
        y = xh * gain[...] + shift[...]
        hat[at, :] = xh.astype(BF)
        columns[at, col : col + 1] = rs
        res[at, :] = y
        y_low[at, :] = y.astype(BF)


def norm_grad(dy, xh, rs, gain):
    dx = dy * gain
    return rs * (
        dx - jnp.mean(dx, axis=-1, keepdims=True) - xh * jnp.mean(dx * xh, axis=-1, keepdims=True)
    )


def norm_backward(res, gain, hat, columns, col, g_low, vec, at_gain, at_shift, at_bias):
    rows = res.shape[0]

    @pl.loop(0, rows // BLK)
    def _(i):
        at = tile_at(i, BLK)
        dy = res[at, :]
        xh = hat[at, :].astype(F32)
        g = norm_grad(dy, xh, columns[at, col : col + 1], gain[...])
        low = g.astype(BF)
        res[at, :] = g
        g_low[at, :] = low
        vec[at_gain : at_gain + 1, :] += total(dy * xh)
        vec[at_shift : at_shift + 1, :] += total(dy)
        vec[at_bias : at_bias + 1, :] += total(low)


def head_masks():
    lane = lax.broadcasted_iota(jnp.int32, (1, 128), 1)
    first = (lane < HD).astype(BF)
    return first, (1 - first).astype(BF)


def stack_heads(x, masks):
    return jnp.concatenate([x * masks[0], x * masks[1]], axis=0)


def pick_heads(x):
    lane = lax.broadcasted_iota(jnp.int32, (PAIR, 128), 1)
    return jnp.where(lane < HD, x[:PAIR], x[PAD : PAD + PAIR])


def store_pairs(dst, x, at, first=0):
    zeros = jnp.zeros((PAD - PAIR, x.shape[1]), F32)
    for p in range(x.shape[0] // PAIR):
        block = jnp.concatenate([x[p * PAIR : (p + 1) * PAIR], zeros], axis=0)
        dst[pl.ds(pl.multiple_of((first + p) * PAD, 16), PAD), at] = block.astype(BF)


def probabilities(q2, k, rid, kid):
    s = nt(q2, k) * (1.0 / HD**0.5)
    s = jnp.where(rid == kid, s, -1000000000.0)
    e = jnp.exp(s - jnp.max(s, axis=-1, keepdims=True))
    return e * (1.0 / jnp.sum(e, axis=-1, keepdims=True))


def attention_forward(g, qkv, rid, kids, out):
    masks = head_masks()
    group = pl.ds(pl.multiple_of(g * GR, GR), GR)
    for p in range(H // 2):
        done = []
        for half in range(2):
            rows = pl.ds(pl.multiple_of((2 * g + half) * PAD, 16), PAD)
            q2 = stack_heads(qkv[rows, p * 128 : p * 128 + 128], masks)
            prob = probabilities(q2, qkv[rows, D + p * 128 : D + p * 128 + 128], rid[...], kids[2 * g + half])
            done.append(pick_heads(nn(prob.astype(BF), qkv[rows, 2 * D + p * 128 : 2 * D + p * 128 + 128])))
        out[group, p * 128 : p * 128 + 128] = jnp.concatenate(done, axis=0).astype(BF)


def attention_backward(g, qkv, grad_out, rid, kids, out):
    masks = head_masks()
    group = pl.ds(pl.multiple_of(g * GR, GR), GR)
    for p in range(H // 2):
        done = [[], [], []]
        for half in range(2):
            rows = pl.ds(pl.multiple_of((2 * g + half) * PAD, 16), PAD)
            q2 = stack_heads(qkv[rows, p * 128 : p * 128 + 128], masks)
            k = qkv[rows, D + p * 128 : D + p * 128 + 128]
            v = qkv[rows, 2 * D + p * 128 : 2 * D + p * 128 + 128]
            g2 = stack_heads(grad_out[rows, p * 128 : p * 128 + 128], masks)
            prob = probabilities(q2, k, rid[...], kids[2 * g + half])
            gp = nt(g2, v)
            gv = tn(prob.astype(BF), g2)
            s = prob * (gp - jnp.sum(gp * prob, axis=-1, keepdims=True))
            s = s.astype(BF)
            done[0].append(pick_heads(nn(s, k)) * (1.0 / HD**0.5))
            done[1].append(tn(s, q2)[:PAIR] * (1.0 / HD**0.5))
            done[2].append(gv[:PAIR])
        for part in range(3):
            at = part * D + p * 128
            out[group, at : at + 128] = jnp.concatenate(done[part], axis=0).astype(BF)


def by_item(wide, dst, g):
    items = wide.shape[1] // LR
    for j in range(D // 128):
        got = [wide[j, pl.ds(g * GROUP + i, LR, stride=items), :] for i in range(GROUP)]
        dst[g * GR : (g + 1) * GR, j * 128 : (j + 1) * 128] = jnp.concatenate(got, axis=0).astype(BF)


def widen(src, wide):
    @pl.loop(0, src.shape[0] // BLK)
    def _(i):
        at = tile_at(i, BLK)
        for j in range(D // 128):
            wide[j, at, :] = src[at, j * 128 : (j + 1) * 128].astype(F32)


NAMES = (
    "tokens", "region_mask", "cotangent", "cross_qkv", "cross_q_bias", "cross_v_bias",
    "cross_out", "cross_out_bias", "cross_gain", "cross_shift", "self_qkv", "self_q_bias",
    "self_v_bias", "self_out", "self_out_bias", "self_gain", "self_shift", "ffn_in",
    "ffn_in_bias", "ffn_out", "ffn_out_bias", "ffn_gain", "ffn_shift",
)
SMALL = tuple(n for n in NAMES if n.endswith(("bias", "gain", "shift")))
NS = len(SMALL)
KINDS = ((4 * BLK, TILE), (BLK, 1024), (BLK, D))
PARTS = (
    *((0, TILE * i, 0) for i in range(3)),
    *((1, 1024 * i, 1) for i in range(3)),
    (2, 0, 2),
    *((3, D * i, 2) for i in range(3)),
    (4, 0, 2),
    *((5, D * i, 2) for i in range(3)),
)
NP = len(PARTS)
FIRST_CROSS = 10
OUTS = ((4 * BLK, D), (BLK, FF), (BLK, D), (BLK, 3 * D), (BLK, D), (BLK, 3 * D))
HALF = D // 2
BY_Y = (10, 12)
IN_KIND = [sum(p[2] == PARTS[i][2] for p in PARTS[:i]) for i in range(NP)]
COUNT = [sum(p[2] == k for p in PARTS) for k in range(3)]


SERVE = {
    -3: (100,),
    20: (101,),
    21: (102,),
    4: (200,),
    -6: (103,),
    30: (104, 201, 105, 300,),
    40: (202, 301, 106,),
    41: (400,),
    43: (203, 302,),
    7: (401,),
    -10: (107,),
    9: (204,),
    33: (108, 303, 109, 402,),
    10: (304, 205,),
    35: (403,),
    50: (110, 206, 404,),
    51: (305,),
    52: (207, 306,),
    53: (405,),
    11: (208,),
    12: (307, 510,),
    -14: (111,),
    13: (406,),
    36: (112, 209,),
    60: (308, 113, 210, 407, 309,),
    61: (211, 408, 310, 409, 311, 512,),
    62: (213, 410, 411, 610, 212, 313,),
    63: (312, 611, 413, 412, 613, 612,),
}


def body(fused, *refs):
    refs = list(refs)

    def take(n):
        got = refs[:n]
        del refs[:n]
        return got

    tok_h, far_h, cot_h, cqkv_h, cout_h, sqkv_h, sout_h, fin_h, fout_h = take(9)
    (mask_in,) = take(1)
    given = dict(zip(SMALL, take(NS)))
    out_o, grad_o, back_o, vec_o = take(4)
    parts_o = take(len(OUTS) if fused else NP)
    (tok, far, cot, wp, wq, xqkv, xatt, joined, hat1, sqkv, satt, settled, hat2, active, inner,
     res, g_low, gpad, rid, columns, slot_a, slot_b, kid_own, kid_far, sv,
     out_f, sems, part_sems) = take(28)
    rows = tok.shape[0]
    groups = rows // GR
    gx = active
    side = lax.axis_index("stream")

    def fetch(i, src, dst):
        c = pltpu.make_async_copy(src, dst, sems.at[i])
        c.start()
        return c

    if fused:
        acc, xr, za, zb, fin = take(3), take(3), take(3), take(3), take(3)
        yr, back, vbuf, ybf = take(4)
        s_core, r_core, s_x, r_x, s_za, r_za, s_zb, r_zb, s_y, r_y, s_yf, r_yf, s_m, r_m = take(14)
        me = lax.axis_index("dp")
        core, x = lax.rem(me, 2), lax.rem(lax.div(me, 2), 2)
        zl, zh = lax.rem(lax.div(me, 4), 2), lax.div(me, 8)
        to_y, to_core = (1 - side, me), (side, me + 1 - 2 * core)
        to_x, to_zl, to_zh = (side, me + 2 - 4 * x), (side, me + 4 - 8 * zl), (side, me + 8 - 16 * zh)
        peers = (to_y, to_core, to_x, to_zl, to_zh)
        def remote(src, dst, send, recv, peer):
            return pltpu.make_async_remote_copy(
                src_ref=src, dst_ref=dst, send_sem=send, recv_sem=recv,
                device_id=peer, device_id_type=pl.DeviceIdType.MESH,
            )

    c_tok = fetch(0, tok_h, g_low)
    c_cqkv = fetch(1, cqkv_h, wp.at[:, 0 : 3 * D])
    c_cot = fetch(8, cot_h, settled)
    c_cout = fetch(3, cout_h, wp.at[:, 3 * D :])
    if not fused:
        c_far = fetch(2, far_h, satt)

    def fetch_self():
        return [
            *(fetch(4 + j, sqkv_h.at[:, j * D : (j + 1) * D], wq.at[j * D : (j + 1) * D, :]) for j in range(3)),
            fetch(7, sout_h, wq.at[3 * D :, :]),
        ]

    c_self = fetch_self()
    c_tok.wait()
    widen(g_low, out_f)
    if fused:
        barrier = pltpu.get_barrier_semaphore()
        for p in peers:
            pl.semaphore_signal(barrier, inc=1, device_id=p, device_id_type=pl.DeviceIdType.MESH)
        pl.semaphore_wait(barrier, len(peers))

        def tokens_to(g):
            at = pl.ds(pl.multiple_of(g * GR, GR), GR)
            return remote(tok.at[at, :], far.at[at, :], s_m.at[g], r_m.at[g], to_y)

    for g in range(groups):
        by_item(out_f, tok, g)
        if fused:
            tokens_to(g).start()

    sm = SimpleNamespace()
    for i, n in enumerate(SMALL):
        row_of = given[n]
        if len(given[n].shape) == 1:
            sv[i : i + 1, :] = given[n][...].reshape(1, D)
            row_of = sv.at[i : i + 1, :]
        setattr(sm, n, row_of)
    vec = vbuf.at[0] if fused else vec_o
    vec[...] = jnp.zeros(vec.shape, F32)
    edge = lax.broadcasted_iota(jnp.int32, (2 * PAD, PAD), 0)
    second = ((edge >= LR) & (edge < PAD)) | (edge >= PAD + LR)
    rid[...] = second.astype(F32)
    items = rows // LR
    present = (mask_in[...] > 0).astype(F32)
    word = (lax.broadcasted_iota(jnp.int32, (items, LR), 1) < LW).astype(F32)
    slot = lax.broadcasted_iota(jnp.int32, (LR, GR), 0)
    lane = lax.broadcasted_iota(jnp.int32, (1, GR), 1)
    lane_item = sum((lane >= LR * i).astype(jnp.int32) for i in range(1, GROUP))
    spread_slots = (slot == lane - LR * lane_item).astype(BF)
    row = lax.broadcasted_iota(jnp.int32, (GR, GR), 0)
    diagonal = row == lax.broadcasted_iota(jnp.int32, (GR, GR), 1)

    def lay_masks(mask, kid, own):
        spread = nn(mask.astype(BF), spread_slots)
        for g in range(groups):
            line = jnp.zeros((1, GR), F32)
            for i in range(GROUP):
                line += jnp.where(lane_item == i, spread[g * GROUP + i : g * GROUP + i + 1, :], 0.0)
            ids = jnp.where(line > 0.5, (lane_item % 2).astype(F32), -1.0)
            for half in range(2):
                kid[2 * g + half, :, 0:PAIR] = ids[:, half * PAIR : (half + 1) * PAIR]
                kid[2 * g + half, :, PAIR:] = jnp.full((1, PAD - PAIR), -1.0, F32)
            if own:
                column = jnp.sum(jnp.where(diagonal, line, 0.0), axis=-1, keepdims=True)
                columns[g * GR : (g + 1) * GR, 0:1] = column

    lay_masks(jnp.where(side == 0, word, present), kid_own, True)
    lay_masks(jnp.where(side == 0, present, word), kid_far, False)

    c_cqkv.wait()

    @pl.loop(0, 3)
    def _(j):
        at = tile_at(j)
        store_pairs(xqkv, nn(tok[...], wp[:, at]) + sm.cross_q_bias[:, at], at)

    c_cot.wait()
    widen(settled, out_f)
    for g in range(groups):
        by_item(out_f, cot, g)
    if not fused:
        c_far.wait()
        widen(satt, out_f)
        for g in range(groups):
            by_item(out_f, far, g)

    @pl.loop(0, groups)
    def _(g):
        at_g = pl.ds(pl.multiple_of(g * GR, GR), GR)
        if fused:
            tokens_to(g).wait_recv()
        x = far[at_g, :]
        for j in range(3, 9):
            y = nn(x, wp[:, j * TILE : (j + 1) * TILE])
            if j >= 6:
                y = y + sm.cross_v_bias[:, (j - 6) * TILE : (j - 5) * TILE]
            store_pairs(xqkv, y, slice(j * TILE, (j + 1) * TILE), 2 * g)
        attention_forward(g, xqkv, rid, kid_far, xatt)

    c_cout.wait()

    @pl.loop(0, 3)
    def _(j):
        at = tile_at(j)
        w_at = pl.ds(pl.multiple_of(3 * D + j * TILE, TILE), TILE)
        res[:, at] = tok[:, at].astype(F32) + nn(xatt[...], wp[:, w_at]) + sm.cross_out_bias[:, at]

    c_fin = fetch(1, fin_h, wp)
    norm_forward(res, sm.cross_gain, sm.cross_shift, hat1, columns, 1, joined)

    for c in c_self:
        c.wait()
    for part in range(3):
        @pl.loop(0, 3)
        def _(j):
            at = tile_at(j)
            x = nn(joined[...], wq[part * D : (part + 1) * D, at])
            if part == 0:
                x = x + sm.self_q_bias[:, at]
            if part == 2:
                x = x + sm.self_v_bias[:, at]
            store_pairs(sqkv, x, pl.ds(pl.multiple_of(part * D + j * TILE, TILE), TILE))

    @pl.loop(0, groups)
    def _(g):
        attention_forward(g, sqkv, rid, kid_own, satt)

    @pl.loop(0, 3)
    def _(j):
        at = tile_at(j)
        res[:, at] += nn(satt[...], wq[3 * D :, at]) + sm.self_out_bias[:, at]

    c_fout = fetch(3, fout_h, wq)
    norm_forward(res, sm.self_gain, sm.self_shift, hat2, columns, 2, settled)

    c_fin.wait()

    @pl.loop(0, FF // TILE)
    def _(j):
        at = tile_at(j)
        x = nn(settled[...], wp[:, at]) + sm.ffn_in_bias[:, at]
        half = 0.5 * (1.0 + lax.erf(x * (0.5**0.5)))
        active[:, at] = (x * half).astype(BF)
        inner[:, at] = (half + x * jnp.exp(-0.5 * x * x) * 0.3989422804014327).astype(BF)

    c_fout.wait()

    @pl.loop(0, 3)
    def _(j):
        at = tile_at(j)
        res[:, at] += nn(active[...], wq[:, at]) + sm.ffn_out_bias[:, at]

    @pl.loop(0, rows // BLK)
    def _(i):
        at = tile_at(i, BLK)
        r = res[at, :]
        ok = columns[at, 0:1]
        gain = sm.ffn_gain[...]
        centre = r - jnp.mean(r, axis=-1, keepdims=True)
        rs = lax.rsqrt(jnp.mean(centre * centre, axis=-1, keepdims=True) + 1e-12)
        xh = centre * rs
        y = xh * gain + sm.ffn_shift[...]
        for j in range(D // 128):
            out_f[j, at, :] = y[:, j * 128 : (j + 1) * 128] * ok
        dy = cot[at, :].astype(F32) * ok
        g = norm_grad(dy, xh, rs, gain)
        low = g.astype(BF)
        res[at, :] = g
        cot[at, :] = low
        vec[FGAIN : FGAIN + 1, :] += total(dy * xh)
        vec[FSHIFT : FSHIFT + 1, :] += total(dy)
        vec[FOUTB : FOUTB + 1, :] += total(low)

    c_out = fetch(8, out_f, out_o)

    def slot_of(i):
        kind = PARTS[i][2]
        if kind == 0:
            return slot_b.at[i % 2]
        ref = slot_a.at[i % 2]
        return ref if kind == 1 else ref.at[:, :, :, :, :, 0:D]

    mv = SimpleNamespace(
        core={}, y={}, x={}, zl={}, zh={}, yf={}, out={}, acc={}, rx={}, rza={}, rzb={}, fin={}
    )
    out_going, far_going = [], []
    if fused:
        for i in range(NP):
            out, col, kind = PARTS[i]
            n = IN_KIND[i]
            a, width = acc[kind].at[n], KINDS[kind][1]
            mv.core[i] = remote(slot_of(i).at[1 - core], a, s_core.at[i], r_core.at[i], to_core)
            r_xi, r_zai, r_zbi = xr[kind].at[n], za[kind].at[n], zb[kind].at[n]
            if i in BY_Y:
                c = i - FIRST_CROSS
                mine = pl.ds(pl.multiple_of(side * HALF, HALF), HALF)
                other = pl.ds(pl.multiple_of((1 - side) * HALF, HALF), HALF)
                mv.y[i] = remote(a.at[:, :, :, :, other], yr.at[c], s_y.at[c], r_y.at[c], to_y)
                a = a.at[:, :, :, :, mine]
                cut = pl.ds(0, HALF)
                r_xi, r_zai, r_zbi = r_xi.at[:, :, :, cut], r_zai.at[:, :, cut], r_zbi.at[:, cut]
                width = HALF
            mv.acc[i], mv.rx[i], mv.rza[i], mv.rzb[i] = a, r_xi, r_zai, r_zbi
            mv.x[i] = remote(a.at[:, :, 1 - x], r_xi, s_x.at[i], r_x.at[i], to_x)
            mv.zl[i] = remote(a.at[:, 1 - zl, x], r_zai, s_za.at[i], r_za.at[i], to_zl)
            mv.zh[i] = remote(a.at[1 - zh, zl, x], r_zbi, s_zb.at[i], r_zb.at[i], to_zh)
            f = fin[kind].at[n % 2]
            if i in BY_Y:
                f = f.at[:, 0:HALF]
                col0 = pl.ds(pl.multiple_of(col + side * HALF, HALF), HALF)
            else:
                col0 = pl.ds(col, width)
            mv.fin[i] = f
            mv.out[i] = pltpu.make_async_copy(f, parts_o[out].at[:, col0], part_sems.at[i])
            if i in BY_Y:
                mv.yf[i] = remote(f, parts_o[out].at[:, col0], s_yf.at[c], r_yf.at[c], to_y)
            elif i >= FIRST_CROSS:
                c = i - FIRST_CROSS
                mv.yf[i] = remote(ybf.at[c // 2, 0], ybf.at[c // 2, 1], s_yf.at[c], r_yf.at[c], to_y)

        def t1(i):
            mv.core[i].wait_recv()
            out, col, kind = PARTS[i]
            a, own = acc[kind].at[IN_KIND[i]], slot_of(i)

            @pl.loop(0, 8)
            def _(d):
                p, q, r = lax.div(d, 4), lax.rem(lax.div(d, 2), 2), lax.rem(d, 2)
                a[p, q, r] = a[p, q, r] + own[core, p, q, r]

            (mv.y if i in BY_Y else mv.x)[i].start()

        def ty(i):
            mv.y[i].wait_recv()
            a, c = mv.acc[i], i - FIRST_CROSS

            @pl.loop(0, 8)
            def _(d):
                p, q, r = lax.div(d, 4), lax.rem(lax.div(d, 2), 2), lax.rem(d, 2)
                a[p, q, r] = a[p, q, r] + yr[c, p, q, r]

            mv.x[i].start()

        def t2(i):
            mv.x[i].wait_recv()
            a, r = mv.acc[i], mv.rx[i]

            @pl.loop(0, 4)
            def _(d):
                p, q = lax.div(d, 2), lax.rem(d, 2)
                a[p, q, x] = a[p, q, x] + r[p, q]

            mv.zl[i].start()

        def t3(i):
            mv.zl[i].wait_recv()
            a, r = mv.acc[i], mv.rza[i]
            for p in range(2):
                a[p, zl, x] = a[p, zl, x] + r[p]
            mv.zh[i].start()

        def room(i):
            before = [j for j in range(i) if PARTS[j][2] == PARTS[i][2] and IN_KIND[j] == IN_KIND[i] - 2]
            for j in before:
                mv.out[j].wait()
                out_going.remove(j)
                if j in BY_Y:
                    mv.yf[j].wait_send()
                    far_going.remove(j)

        def t4(i):
            mv.zh[i].wait_recv()
            whole = mv.acc[i][zh, zl, x].astype(F32) + mv.rzb[i][...].astype(F32)
            if i >= FIRST_CROSS and i not in BY_Y:
                ybf[(i - FIRST_CROSS) // 2, 0] = whole.astype(BF)
                mv.yf[i].start()
                far_going.append(i)
                return
            room(i)
            mv.fin[i][...] = whole
            mv.out[i].start()
            out_going.append(i)
            if i in BY_Y:
                mv.yf[i].start()
                far_going.append(i)

        def tf(i):
            mv.yf[i].wait_recv()
            if i not in BY_Y:
                room(i)
                c = i - FIRST_CROSS
                mv.fin[i][...] = ybf[c // 2, 0].astype(F32) + ybf[c // 2, 1].astype(F32)
                mv.out[i].start()
                out_going.append(i)

        steps = (t1, t2, t3, t4, ty, tf)
    left = []
    for i in range(NP):
        left += [n * 100 + i for n in (1, 2, 3, 4) + (5,) * (i in BY_Y) + (6,) * (i >= FIRST_CROSS)]
    core_free = {}

    def serve(place):
        if fused:
            for t in SERVE.get(place, ()):
                left.remove(t)
                steps[t // 100 - 1](t % 100)

    def free_slot(i):
        if i in core_free:
            core_free.pop(i)()

    def push(i):
        if fused:
            mv.core[i].start()
            core_free[i] = mv.core[i].wait_send
        else:
            c = pltpu.make_async_copy(slot_of(i), parts_o[i], part_sems.at[i])
            c.start()
            core_free[i] = c.wait

    def same_slot(i):
        for j in range(i - 1, -1, -1):
            if (PARTS[j][2] == 0) == (PARTS[i][2] == 0) and j % 2 == i % 2:
                return j
        return None

    def weight_part(i, left, right, col0):
        serve(-1 - i)
        free_slot(same_slot(i))
        ref = slot_of(i)
        width = KINDS[PARTS[i][2]][1]

        @pl.loop(0, width // TILE)
        def _(j):
            src = right[:, pl.ds(pl.multiple_of(col0 + j * TILE, TILE), TILE)]
            w = tn(left[...], src).astype(BF)
            for d in range(16):
                ref[d % 2, d // 8, (d // 4) % 2, (d // 2) % 2, :, tile_at(j)] = w[d * BLK : (d + 1) * BLK, :]

        push(i)
        serve(i)

    for col in range(3):
        serve(-1 - col)
        free_slot(same_slot(col))
        ref = slot_of(col)

        @pl.loop(0, 4)
        def _(t):
            w = tn(active[:, tile_at(t, D)], cot[:, col * TILE : (col + 1) * TILE]).astype(BF)
            for d in range(4):
                ref[d % 2, lax.div(t, 2), lax.rem(t, 2), d // 2, :, :] = w[d * 4 * BLK : (d + 1) * 4 * BLK, :]

        push(col)
        serve(col)

    for r in range(3):
        @pl.loop(4 * r, 4 * r + 4)
        def _(j):
            at = tile_at(j)
            ga = nt(cot[...], wq[at, :])
            gi = (ga * inner[:, at].astype(F32)).astype(BF)
            inner[:, at] = gi

        serve(20 + r)
    for r in range(4):
        vec[FINB + r : FINB + r + 1, :] = total(inner[:, r * D : (r + 1) * D])
    c_self = fetch_self()

    for col in range(3):
        weight_part(3 + col, settled, inner, col * 1024)

    @pl.loop(0, 3)
    def _(j):
        at = tile_at(j)
        res[:, at] += nt(inner[...], wp[at, :])

    serve(30)
    c_cqkv = fetch(1, cqkv_h, wp.at[:, 0 : 3 * D])
    c_cout = fetch(3, cout_h, wp.at[:, 3 * D :])
    norm_backward(res, sm.self_gain, hat2, columns, 2, g_low, vec, SGAIN, SSHIFT, SOUTB)
    serve(31)
    weight_part(6, satt, g_low, 0)
    for c in c_self:
        c.wait()

    @pl.loop(0, 3)
    def _(j):
        at = tile_at(j)
        w_at = pl.ds(pl.multiple_of(3 * D + j * TILE, TILE), TILE)
        store_pairs(gpad, nt(g_low[...], wq[w_at, :]), at)

    serve(32)

    def serve_each(place, g):
        for k in range(groups):
            if fused and SERVE.get(place + k):
                @pl.when(g == k)
                def _():
                    serve(place + k)

    @pl.loop(0, groups)
    def _(g):
        attention_backward(g, sqkv, gpad, rid, kid_own, gx)
        serve_each(40, g)

    for part in range(3):
        weight_part(7 + part, joined, gx, part * D)
    vec[SQB : SQB + 1, :] = total(gx[:, 0:D])
    vec[SVB : SVB + 1, :] = total(gx[:, 2 * D : 3 * D])

    @pl.loop(0, 3)
    def _(j):
        at = tile_at(j)
        g = res[:, at]
        for part in range(3):
            w_at = pl.ds(pl.multiple_of(part * D + j * TILE, TILE), TILE)
            g += nt(gx[:, part * D : (part + 1) * D], wq[w_at, :])
        res[:, at] = g

    serve(33)
    norm_backward(res, sm.cross_gain, hat1, columns, 1, g_low, vec, CGAIN, CSHIFT, COUTB)
    serve(34)
    weight_part(10, xatt, g_low, 0)
    c_cqkv.wait()
    c_cout.wait()

    @pl.loop(0, 3)
    def _(j):
        at = tile_at(j)
        store_pairs(gpad, nt(g_low[...], wp[at, 3 * D :]), at)

    serve(35)
    if fused:

        def back_to(g):
            at = pl.ds(pl.multiple_of(g * GR, GR), GR)
            return remote(g_low.at[at, :], back.at[at, :], s_m.at[groups + g], r_m.at[groups + g], to_y)

    @pl.loop(0, groups)
    def _(g):
        attention_backward(g, xqkv, gpad, rid, kid_far, gx)
        at = pl.ds(pl.multiple_of(g * GR, GR), GR)
        pair = gx[at, D : 3 * D]
        for j in range(3):
            w_at = slice(j * TILE, (j + 1) * TILE)
            g_low[at, w_at] = nt(pair, wp[w_at, D : 3 * D]).astype(BF)
        if fused:
            back_to(g).start()
        serve_each(50, g)

    vec[CQB : CQB + 1, :] = total(gx[:, 0:D])
    vec[CVB : CVB + 1, :] = total(gx[:, 2 * D : 3 * D])
    if fused:
        v_at = [
            remote(vbuf.at[j], vbuf.at[4 + j], s_m.at[2 * groups + j], r_m.at[2 * groups + j], p)
            for j, p in enumerate((to_core, to_x, to_zl, to_zh))
        ]
        v_y = remote(vbuf.at[8], vbuf.at[9], s_m.at[2 * groups + 4], r_m.at[2 * groups + 4], to_y)

        def vec_step(j):
            v_at[j].wait_recv()
            if j < 3:
                vbuf[j + 1] = vbuf[j] + vbuf[4 + j]
                v_at[j + 1].start()
            else:
                vbuf[8] = vbuf[3] + vbuf[7]
                v_y.start()

        v_at[0].start()
    weight_part(11, tok, gx, 0)
    weight_part(12, far, gx, D)
    if fused:
        vec_step(0)
    weight_part(13, far, gx, 2 * D)

    @pl.loop(0, 3)
    def _(j):
        at = tile_at(j)
        res[:, at] += nt(gx[:, 0:D], wp[at, 0:D])

    if not fused:
        c_back = fetch(2, g_low, back_o)
        c_grad = fetch(0, res, grad_o)
        for done in core_free.values():
            done()
        c_back.wait()
        c_grad.wait()
        c_out.wait()
        return

    serve(36)
    vec_step(1)
    serve(60)
    for g in range(groups):
        back_to(g).wait()

    @pl.loop(0, rows // BLK)
    def _(i):
        at = tile_at(i, BLK)
        res[at, :] = res[at, :] + back[at, :].astype(F32)

    c_grad = fetch(0, res, grad_o)
    serve(61)
    vec_step(2)
    serve(62)
    vec_step(3)
    serve(63)
    v_y.wait_recv()
    vec_o[...] = vbuf[8]
    vec_o[12:, :] = vbuf[8, 12:, :] + vbuf[9, 12:, :]
    for done in core_free.values():
        done()
    for i in range(NP):
        if i in BY_Y:
            mv.y[i].wait_send()
        for m in (mv.x, mv.zl, mv.zh):
            m[i].wait_send()
    for i in out_going:
        mv.out[i].wait()
    for i in far_going:
        mv.yf[i].wait_send()
    for v in v_at:
        v.wait_send()
    v_y.wait_send()
    for g in range(groups):
        tokens_to(g).wait_send()
    c_out.wait()
    c_grad.wait()
    assert not left


def compute(rows, fused, arrays):
    any_space = pl.BlockSpec(memory_space=pl.ANY)
    vmem = pl.BlockSpec(memory_space=pltpu.VMEM)
    if fused:
        out_parts = [jax.ShapeDtypeStruct(o, F32) for o in OUTS]
    else:
        out_parts = [jax.ShapeDtypeStruct((2, 2, 2, 2, *KINDS[k]), BF) for _, _, k in PARTS]
    low = lambda n=D: pltpu.VMEM((rows, n), BF)
    wide = lambda n: pltpu.VMEM((rows // PAIR * PAD, n), BF)
    dma = lambda n: pltpu.SemaphoreType.DMA((n,))
    scratch = [
        low(), low(), low(),
        pltpu.VMEM((D, FF), BF), pltpu.VMEM((FF, D), BF),
        wide(3 * D), low(), low(), low(),
        wide(3 * D), low(), low(), low(),
        low(FF), low(FF),
        pltpu.VMEM((rows, D), F32), low(), wide(D),
        pltpu.VMEM((2 * PAD, PAD), F32),
        pltpu.VMEM((rows, 128), F32),
        pltpu.VMEM((2, 2, 2, 2, 2, BLK, 1024), BF), pltpu.VMEM((2, 2, 2, 2, 2, 4 * BLK, TILE), BF),
        pltpu.VMEM((rows // PAIR, 1, PAD), F32), pltpu.VMEM((rows // PAIR, 1, PAD), F32),
        pltpu.VMEM((8, D), F32),
        pltpu.VMEM((D // 128, rows, 128), F32),
        dma(9), dma(NP),
    ]
    params = dict(vmem_limit_bytes=int(63.9 * 2**20))
    if fused:
        for lead in ((2, 2, 2), (2, 2), (2,), ()):
            scratch += [pltpu.VMEM((COUNT[k], *lead, *KINDS[k]), BF) for k in range(3)]
        scratch += [pltpu.VMEM((2, *KINDS[k]), F32) for k in range(3)]
        cross = NP - FIRST_CROSS
        scratch += [
            pltpu.VMEM((cross, 2, 2, 2, BLK, HALF), BF), low(), pltpu.VMEM((10, NV, D), F32),
            pltpu.VMEM((cross // 2, 2, BLK, D), BF),
            *([dma(NP)] * 8), *([dma(cross)] * 4), dma(2 * rows // GR + 5), dma(2 * rows // GR + 5),
        ]
        params.update(collective_id=0, has_side_effects=True)
    return pl.pallas_call(
        partial(body, fused),
        out_shape=[
            jax.ShapeDtypeStruct((D // 128, rows, 128), F32),
            jax.ShapeDtypeStruct((rows, D), F32),
            jax.ShapeDtypeStruct((8, 128) if fused else (rows, D), BF),
            jax.ShapeDtypeStruct((NV, D), F32),
            *out_parts,
        ],
        in_specs=[any_space] * 9 + [vmem] * (1 + NS),
        out_specs=[any_space] * 3 + [vmem] + [any_space] * len(out_parts),
        scratch_shapes=scratch,
        compiler_params=pltpu.CompilerParams(**params),
    )(*arrays)


VECTORS = (CQB, CVB, COUTB, CGAIN, CSHIFT, SQB, SVB, SOUTB, SGAIN, SSHIFT, FOUTB, FGAIN, FSHIFT)


def finish_body(n, copies, *refs):
    refs = list(refs)

    def take(count):
        got = refs[:count]
        del refs[:count]
        return got

    stream_h, grad_h, vec = take(3)
    sums = take(copies)
    stream_o, grad_o = take(2)
    vectors = take(len(VECTORS))
    (finb,) = take(1)
    sums_o = take(copies)
    stream, grad, wide, stream_t, grad_t, sems = take(6)
    held = take(copies)
    items = grad.shape[0] // LR
    c_grad = pltpu.make_async_copy(grad_h, grad, sems.at[0])
    c_stream = pltpu.make_async_copy(stream_h, stream, sems.at[1])
    c_grad.start()
    c_stream.start()
    into = [pltpu.make_async_copy(a, b, sems.at[2 + i]) for i, (a, b) in enumerate(zip(sums, held))]
    out = [pltpu.make_async_copy(a, b, sems.at[2 + i]) for i, (a, b) in enumerate(zip(held, sums_o))]
    for c in into:
        c.start()
    me = lax.axis_index("dp")
    share = D // n
    mine = pltpu.roll(vec[...], lax.rem(D - me * share, D), 1)
    for r, v in zip(VECTORS, vectors):
        v[...] = mine[r : r + 1, 0:share].reshape(v.shape)
    share = FF // n
    a_row = D // share
    v = vec[FINB : FINB + 8, :]
    at = lax.broadcasted_iota(jnp.int32, v.shape, 0) == lax.div(me, a_row)
    line = jnp.broadcast_to(jnp.sum(jnp.where(at, v, 0.0), axis=0, keepdims=True), v.shape)
    finb[...] = pltpu.roll(line, lax.rem(D - lax.rem(me, a_row) * share, D), 1)[0:1, 0:share]
    c_grad.wait()
    for j in range(D // 128):
        cols = slice(j * 128, (j + 1) * 128)
        for i in range(items):
            wide[0, j, pl.ds(i, LR, stride=items), :] = grad[i * LR : (i + 1) * LR, cols]
        grad_t[:, cols] = wide[0, j]
    c_grad = pltpu.make_async_copy(grad_t, grad_o, sems.at[0])
    c_grad.start()
    for a, b in zip(into, out):
        a.wait()
        b.start()
    c_stream.wait()
    for j in range(D // 128):
        cols = slice(j * 128, (j + 1) * 128)
        for i in range(items):
            wide[1, j, pl.ds(i, LR, stride=items), :] = stream[j, i * LR : (i + 1) * LR, :]
        stream_t[:, cols] = wide[1, j].astype(BF)
    c_stream = pltpu.make_async_copy(stream_t, stream_o, sems.at[1])
    c_stream.start()
    for c in out:
        c.wait()
    c_grad.wait()
    c_stream.wait()


def finish(n, stream, grad, vec, sums):
    any_space = pl.BlockSpec(memory_space=pl.ANY)
    vmem = pl.BlockSpec(memory_space=pltpu.VMEM)
    share = D // n
    shapes = [(share,)] * 5 + [(1, share)] * 8 + [(1, FF // n)]
    return pl.pallas_call(
        partial(finish_body, n, len(sums)),
        out_shape=[
            jax.ShapeDtypeStruct(grad.shape, BF),
            jax.ShapeDtypeStruct(grad.shape, F32),
            *(jax.ShapeDtypeStruct(s, F32) for s in shapes),
            *(jax.ShapeDtypeStruct(x.shape, F32) for x in sums),
        ],
        in_specs=[any_space] * 2 + [vmem] + [any_space] * len(sums),
        out_specs=[any_space] * 2 + [vmem] * len(shapes) + [any_space] * len(sums),
        scratch_shapes=[
            pltpu.VMEM(stream.shape, F32), pltpu.VMEM(grad.shape, F32), pltpu.VMEM((2, *stream.shape), F32),
            pltpu.VMEM(grad.shape, BF), pltpu.VMEM(grad.shape, F32),
            pltpu.SemaphoreType.DMA((2 + len(sums),)),
            *(pltpu.VMEM(x.shape, F32) for x in sums),
        ],
        compiler_params=pltpu.CompilerParams(vmem_limit_bytes=int(63.9 * 2**20)),
    )(stream, grad, vec, *sums)


def partner(block):
    return lax.ppermute(block, "stream", [(0, 1), (1, 0)])


def reduce_parts(parts, vec):
    def natural(some):
        done = []
        for p in some:
            r, n = p.shape[-2:]
            done.append(p.transpose(1, 2, 3, 0, 4, 5).reshape(16 * r, n))
        return jnp.concatenate(done, axis=1)

    def scatter(some, shared=False):
        x = natural(some)
        if shared:
            x = lax.psum(x, "stream")
        return lax.psum_scatter(x, "dp", scatter_dimension=0, tiled=True).astype(F32)

    sums = [
        scatter(parts[0:3]), scatter(parts[3:6]), scatter(parts[6:7]), scatter(parts[7:10]),
        scatter(parts[10:11], True), scatter(parts[11:14], True),
    ]
    own = lax.psum(vec[:CGAIN], "dp")
    return sums, jnp.concatenate([own, lax.psum(vec[CGAIN:], ("stream", "dp"))])


def local(*args):
    a = dict(zip(NAMES, args))
    n = lax.axis_size("dp")
    fused = n == 16
    shape = a["tokens"].shape
    items = shape[1]

    def by_slot(v):
        return v[0].transpose(1, 0, 2).reshape(items * LR, D)

    def back_to_items(v):
        return v.reshape(LR, items, D).transpose(1, 0, 2).reshape(shape)

    tok, cot = by_slot(a["tokens"]), by_slot(a["cotangent"])
    far = tok if fused else partner(tok)
    outs = compute(
        items * LR,
        fused,
        [tok, far, cot, a["cross_qkv"], a["cross_out"], a["self_qkv"][0], a["self_out"][0],
         a["ffn_in"][0], a["ffn_out"][0], a["region_mask"], *(a[k] for k in SMALL)],
    )
    stream, grad, back, vec = outs[:4]
    sums = outs[4:]
    if not fused:
        grad = grad + partner(back).astype(F32)
        sums, vec = reduce_parts(sums, vec)
    done = finish(n, stream, grad, vec, sums if fused else [])
    if fused:
        sums = done[16:]
    fout, fin, sout, sqkv, cout, cqkv = sums
    cqb, cvb, coutb, cgain, cshift, sqb, svb, soutb, sgain, sshift, foutb, fgain, fshift, finb = done[2:16]
    return (
        back_to_items(done[0]), back_to_items(done[1]),
        cqkv, cqb, cvb, cout, coutb, cgain, cshift,
        sqkv[None], sqb, svb, sout[None], soutb, sgain, sshift,
        fin[None], finb, fout[None], foutb, fgain, fshift,
    )


def solution(mesh):
    both = P("stream", "dp")
    one = P("stream")
    specs = {n: one for n in NAMES}
    specs.update({n: P() for n in NAMES if n.startswith("cross")})
    specs.update(tokens=both, cotangent=both, region_mask=P("dp"))
    return jax.shard_map(
        local,
        mesh=mesh,
        in_specs=tuple(specs[n] for n in NAMES),
        out_specs=(both, both) + (P("dp"),) * 7 + (both,) * 13,
        check_vma=False,
    )
```

time: 612 us -> 196 us (0.32)
  waiting for transfers between devices: 315 us -> 0 us
  blocking collectives: 95.6 us -> 0 us
  Pallas kernels: 123 us -> 194 us
  local copies, waits for them, and re-layouts: 36.9 us -> 0 us
  other arithmetic: 22.2 us -> 0 us
  between operations: 14.5 us -> 0.86 us
    reduce_scatter x6 -> x0, waiting for transfers between devices: 278 us -> none  [scatter(): lax.psum_scatter(x, 'dp', scatter_dimension=0, tiled=True).astype(F32)]
    psum x2 -> x0, blocking collectives: 95.6 us -> none  [the longest x1 57.7 us: local(): own_vec = lax.psum(vec[:12], 'dp')]
    pallas_call x1 -> x2, Pallas kernels: 123 us -> 194 us  [the longest x1 188 us: compute(): pl.pallas_call(partial(body, fused), out_shape=[jax.ShapeDtypeStruct((D /...]
    psum x1 -> x0, waiting for transfers between devices: 23.3 us -> none  [scatter(): x = lax.psum(x, 'stream')]
    unnamed x50 -> x0, local copies, waits for them, and re-layouts: 14.4 us -> none
    ppermute x2 -> x0, waiting for transfers between devices: 13.7 us -> none  [partner(): return lax.ppermute(block, 'stream', [(0, 1), (1, 0)])]
    concatenate x4 -> x0, other arithmetic: 10 us -> none  [natural(): return jnp.concatenate(done, axis=1)]
    dynamic_slice x14 -> x0, local copies, waits for them, and re-layouts: 8.21 us -> none  [the longest x13 7.57 us: mine(): return lax.dynamic_slice_in_dim(v[r], me * (D // n), D // n)]
  transfers between devices with their start and end apart: 9 -> 0, of which waited for: 7 -> 0; matrix products, arithmetic and copies ran while one was open for 7% -> 0% of each run, Pallas kernels for 0% -> 0%
where the time goes in v2:
time: 196 us; the launch traced here: 195 us
  Pallas kernels  194 us (99%)
    pallas_call x1, Pallas kernels, compute(): pl.pallas_call(partial(body, fused), out_shape=[jax.ShapeDtypeStruct((D /...  188 us
    pallas_call x1, Pallas kernels, finish(): pl.pallas_call(partial(finish_body, n, len(sums)), out_shape=[jax.ShapeDt...  6.33 us

profile of v2, /device:TPU:0, one launch (start us, length us, event | category | flops | bytes accessed | tf_op | source)
XLA Modules:
  0.0 195.3 jit_solution(17350095986853780844)
XLA Ops:
  0.7 188.1 %shard_map.390 = (f32[6,576,128]{2,1,0:T(8,128)}, f32[576,768]{1,0:T(8,128)}, bf16[8,128]{1,0:T(8,128)(2,1)}, f32[24,768]{1,0:T(8,128)}, f32[192,768]{1,0:T(8,12...) custom-call(bf16[576,768]{1,0:T(8,128)(2,1)} %bitcast.31, ...), custom_call_target="tpu_custom_call" | custom-call | tf_op jit(solution)/shard_map/pallas_call | solution.py:842
  188.8 6.3 %shard_map.391 = (bf16[576,768]{1,0:T(8,128)(2,1)}, f32[576,768]{1,0:T(8,128)}, f32[48]{0:T(128)}, f32[48]{0:T(128)}, f32[48]{0:T(128)}, /*index=5*/f32[48]{0:T(...) custom-call(f32[6,576,128]{2,1,0:T(8,128)} %get-tuple-element.53.ref, ...), custom_call_target="tpu_custom_call" | custom-call | tf_op jit(solution)/shard_map/pallas_call | solution.py:927

commit v3 on v2

--- a/solution.py
+++ b/solution.py
@@ -22,6 +22,8 @@
 PAD = 80
 TILE = 256
 BLK = 48
+NH = 2
+LNB = 144
 FGAIN, FSHIFT, FOUTB, SGAIN, SSHIFT, SOUTB, SQB, SVB, FINB = 0, 1, 2, 3, 4, 5, 6, 7, 8
 CGAIN, CSHIFT, COUTB, CQB, CVB = 12, 13, 14, 15, 16
 NV = 24
@@ -47,12 +49,10 @@
     return jnp.sum(x.astype(F32), axis=0, keepdims=True)
 
 
-def norm_forward(res, gain, shift, hat, columns, col, y_low):
-    rows = res.shape[0]
-
-    @pl.loop(0, rows // BLK)
+def norm_forward(res, gain, shift, hat, columns, col, y_low, first, count):
+    @pl.loop(0, count // LNB)
     def _(i):
-        at = tile_at(i, BLK)
+        at = pl.ds(pl.multiple_of(first + i * LNB, 16), LNB)
         r = res[at, :]
         centre = r - jnp.mean(r, axis=-1, keepdims=True)
         rs = lax.rsqrt(jnp.mean(centre * centre, axis=-1, keepdims=True) + 1e-12)
@@ -74,9 +74,9 @@
 def norm_backward(res, gain, hat, columns, col, g_low, vec, at_gain, at_shift, at_bias):
     rows = res.shape[0]
 
-    @pl.loop(0, rows // BLK)
+    @pl.loop(0, rows // LNB)
     def _(i):
-        at = tile_at(i, BLK)
+        at = tile_at(i, LNB)
         dy = res[at, :]
         xh = hat[at, :].astype(F32)
         g = norm_grad(dy, xh, columns[at, col : col + 1], gain[...])
@@ -130,9 +130,12 @@
         out[group, p * 128 : p * 128 + 128] = jnp.concatenate(done, axis=0).astype(BF)
 
 
-def attention_backward(g, qkv, grad_out, rid, kids, out):
+def attention_backward(g, qkv, grad_out, columns, col, out):
     masks = head_masks()
     group = pl.ds(pl.multiple_of(g * GR, GR), GR)
+    query = lax.broadcasted_iota(jnp.int32, (1, 2 * PAD), 1)
+    second = ((query >= LR) & (query < PAD)) | (query >= PAD + LR)
+    query_item = second.astype(F32)
     for p in range(H // 2):
         done = [[], [], []]
         for half in range(2):
@@ -141,13 +144,16 @@
             k = qkv[rows, D + p * 128 : D + p * 128 + 128]
             v = qkv[rows, 2 * D + p * 128 : 2 * D + p * 128 + 128]
             g2 = stack_heads(grad_out[rows, p * 128 : p * 128 + 128], masks)
-            prob = probabilities(q2, k, rid[...], kids[2 * g + half])
-            gp = nt(g2, v)
-            gv = tn(prob.astype(BF), g2)
-            s = prob * (gp - jnp.sum(gp * prob, axis=-1, keepdims=True))
+            s = nt(k, q2) * (1.0 / HD**0.5)
+            s = jnp.where(columns[rows, col : col + 1] == query_item, s, -1000000000.0)
+            e = jnp.exp(s - jnp.max(s, axis=0, keepdims=True))
+            prob = e * (1.0 / jnp.sum(e, axis=0, keepdims=True))
+            gp = nt(v, g2)
+            gv = nn(prob.astype(BF), g2)
+            s = prob * (gp - jnp.sum(gp * prob, axis=0, keepdims=True))
             s = s.astype(BF)
-            done[0].append(pick_heads(nn(s, k)) * (1.0 / HD**0.5))
-            done[1].append(tn(s, q2)[:PAIR] * (1.0 / HD**0.5))
+            done[0].append(pick_heads(tn(s, k)) * (1.0 / HD**0.5))
+            done[1].append(nn(s, q2)[:PAIR] * (1.0 / HD**0.5))
             done[2].append(gv[:PAIR])
         for part in range(3):
             at = part * D + p * 128
@@ -159,6 +165,12 @@
     for j in range(D // 128):
         got = [wide[j, pl.ds(g * GROUP + i, LR, stride=items), :] for i in range(GROUP)]
         dst[g * GR : (g + 1) * GR, j * 128 : (j + 1) * 128] = jnp.concatenate(got, axis=0).astype(BF)
+
+
+def by_slot(value, wide, j):
+    items = value.shape[0] // LR
+    for i in range(items):
+        wide[j, pl.ds(i, LR, stride=items), :] = value[i * LR : (i + 1) * LR]
 
 
 def widen(src, wide):
@@ -190,40 +202,54 @@
 FIRST_CROSS = 10
 OUTS = ((4 * BLK, D), (BLK, FF), (BLK, D), (BLK, 3 * D), (BLK, D), (BLK, 3 * D))
 HALF = D // 2
-BY_Y = (10, 12)
 IN_KIND = [sum(p[2] == PARTS[i][2] for p in PARTS[:i]) for i in range(NP)]
 COUNT = [sum(p[2] == k for p in PARTS) for k in range(3)]
 
 
+BY_Y = (10, 12,)
+ORDER = (
+    (2, 1, 0),
+    (1, 2, 0),
+    (2, 1, 0),
+    (1, 0, 2),
+    (2, 1, 0),
+    (2, 1, 0),
+    (2, 1, 0),
+    (2, 1, 0),
+    (2, 1, 0),
+    (2, 1, 0),
+    (2, 1, 0),
+    (2, 1, 0),
+    (2, 1, 0),
+    (2, 1, 0),
+)
 SERVE = {
     -3: (100,),
     20: (101,),
     21: (102,),
-    4: (200,),
     -6: (103,),
-    30: (104, 201, 105, 300,),
-    40: (202, 301, 106,),
-    41: (400,),
-    43: (203, 302,),
-    7: (401,),
+    5: (200,),
+    30: (104, 201,),
+    31: (105,),
+    6: (202,),
+    40: (106, 203,),
+    42: (300, 204,),
+    43: (302,),
+    7: (301,),
     -10: (107,),
-    9: (204,),
-    33: (108, 303, 109, 402,),
-    10: (304, 205,),
-    35: (403,),
-    50: (110, 206, 404,),
-    51: (305,),
-    52: (207, 306,),
-    53: (405,),
-    11: (208,),
-    12: (307, 510,),
+    33: (108, 303,),
+    34: (109, 205, 400,),
+    50: (304, 110, 206,),
+    51: (402, 401,),
+    52: (207, 305,),
+    11: (404,),
+    12: (306, 208,),
     -14: (111,),
-    13: (406,),
-    36: (112, 209,),
-    60: (308, 113, 210, 407, 309,),
-    61: (211, 408, 310, 409, 311, 512,),
-    62: (213, 410, 411, 610, 212, 313,),
-    63: (312, 611, 413, 412, 613, 612,),
+    36: (510, 403, 307, 112,),
+    60: (113, 405, 209, 406, 308, 407,),
+    61: (211, 309, 210, 408, 311, 512, 213,),
+    62: (409, 310, 411, 212, 313, 611,),
+    63: (410, 312, 413, 610, 412, 613, 612,),
 }
 
 
@@ -263,6 +289,10 @@
         to_y, to_core = (1 - side, me), (side, me + 1 - 2 * core)
         to_x, to_zl, to_zh = (side, me + 2 - 4 * x), (side, me + 4 - 8 * zl), (side, me + 8 - 16 * zh)
         peers = (to_y, to_core, to_x, to_zl, to_zh)
+        barrier = pltpu.get_barrier_semaphore()
+        for p in peers:
+            pl.semaphore_signal(barrier, inc=1, device_id=p, device_id_type=pl.DeviceIdType.MESH)
+
         def remote(src, dst, send, recv, peer):
             return pltpu.make_async_remote_copy(
                 src_ref=src, dst_ref=dst, send_sem=send, recv_sem=recv,
@@ -270,25 +300,22 @@
             )
 
     c_tok = fetch(0, tok_h, g_low)
+    def fetch_self():
+        return [
+            *(fetch(4 + j, sqkv_h.at[:, j * D : (j + 1) * D], wq.at[j * D : (j + 1) * D, :]) for j in range(3)),
+            fetch(7, sout_h, wq.at[3 * D :, :]),
+        ]
+
+    c_tok.wait()
     c_cqkv = fetch(1, cqkv_h, wp.at[:, 0 : 3 * D])
     c_cot = fetch(8, cot_h, settled)
     c_cout = fetch(3, cout_h, wp.at[:, 3 * D :])
     if not fused:
         c_far = fetch(2, far_h, satt)
 
-    def fetch_self():
-        return [
-            *(fetch(4 + j, sqkv_h.at[:, j * D : (j + 1) * D], wq.at[j * D : (j + 1) * D, :]) for j in range(3)),
-            fetch(7, sout_h, wq.at[3 * D :, :]),
-        ]
-
     c_self = fetch_self()
-    c_tok.wait()
     widen(g_low, out_f)
     if fused:
-        barrier = pltpu.get_barrier_semaphore()
-        for p in peers:
-            pl.semaphore_signal(barrier, inc=1, device_id=p, device_id_type=pl.DeviceIdType.MESH)
         pl.semaphore_wait(barrier, len(peers))
 
         def tokens_to(g):
@@ -322,7 +349,7 @@
     row = lax.broadcasted_iota(jnp.int32, (GR, GR), 0)
     diagonal = row == lax.broadcasted_iota(jnp.int32, (GR, GR), 1)
 
-    def lay_masks(mask, kid, own):
+    def lay_masks(mask, kid, col, own):
         spread = nn(mask.astype(BF), spread_slots)
         for g in range(groups):
             line = jnp.zeros((1, GR), F32)
@@ -335,9 +362,14 @@
             if own:
                 column = jnp.sum(jnp.where(diagonal, line, 0.0), axis=-1, keepdims=True)
                 columns[g * GR : (g + 1) * GR, 0:1] = column
-
-    lay_masks(jnp.where(side == 0, word, present), kid_own, True)
-    lay_masks(jnp.where(side == 0, present, word), kid_far, False)
+            column = jnp.sum(jnp.where(diagonal, ids, 0.0), axis=-1, keepdims=True)
+            none = jnp.full((PAD - PAIR, 1), -1.0, F32)
+            for half in range(2):
+                padded = jnp.concatenate([column[half * PAIR : (half + 1) * PAIR], none], axis=0)
+                columns[(2 * g + half) * PAD : (2 * g + half + 1) * PAD, col : col + 1] = padded
+
+    lay_masks(jnp.where(side == 0, word, present), kid_own, 3, True)
+    lay_masks(jnp.where(side == 0, present, word), kid_far, 4, False)
 
     c_cqkv.wait()
 
@@ -356,56 +388,67 @@
         for g in range(groups):
             by_item(out_f, far, g)
 
-    @pl.loop(0, groups)
-    def _(g):
-        at_g = pl.ds(pl.multiple_of(g * GR, GR), GR)
-        if fused:
-            tokens_to(g).wait_recv()
-        x = far[at_g, :]
-        for j in range(3, 9):
-            y = nn(x, wp[:, j * TILE : (j + 1) * TILE])
-            if j >= 6:
-                y = y + sm.cross_v_bias[:, (j - 6) * TILE : (j - 5) * TILE]
-            store_pairs(xqkv, y, slice(j * TILE, (j + 1) * TILE), 2 * g)
-        attention_forward(g, xqkv, rid, kid_far, xatt)
-
     c_cout.wait()
-
-    @pl.loop(0, 3)
-    def _(j):
-        at = tile_at(j)
-        w_at = pl.ds(pl.multiple_of(3 * D + j * TILE, TILE), TILE)
-        res[:, at] = tok[:, at].astype(F32) + nn(xatt[...], wp[:, w_at]) + sm.cross_out_bias[:, at]
-
-    c_fin = fetch(1, fin_h, wp)
-    norm_forward(res, sm.cross_gain, sm.cross_shift, hat1, columns, 1, joined)
-
     for c in c_self:
         c.wait()
-    for part in range(3):
+    part_rows, part_groups = rows // NH, groups // NH
+
+    @pl.loop(0, NH)
+    def _(h):
+        first = h * part_rows
+        at_h = pl.ds(pl.multiple_of(first, 16), part_rows)
+
+        @pl.loop(h * part_groups, (h + 1) * part_groups)
+        def _(g):
+            at_g = pl.ds(pl.multiple_of(g * GR, GR), GR)
+            if fused:
+                tokens_to(g).wait_recv()
+            far_g = far[at_g, :]
+            for j in range(3, 9):
+                y = nn(far_g, wp[:, j * TILE : (j + 1) * TILE])
+                if j >= 6:
+                    y = y + sm.cross_v_bias[:, (j - 6) * TILE : (j - 5) * TILE]
+                store_pairs(xqkv, y, slice(j * TILE, (j + 1) * TILE), 2 * g)
+            attention_forward(g, xqkv, rid, kid_far, xatt)
+
         @pl.loop(0, 3)
         def _(j):
             at = tile_at(j)
-            x = nn(joined[...], wq[part * D : (part + 1) * D, at])
-            if part == 0:
-                x = x + sm.self_q_bias[:, at]
-            if part == 2:
-                x = x + sm.self_v_bias[:, at]
-            store_pairs(sqkv, x, pl.ds(pl.multiple_of(part * D + j * TILE, TILE), TILE))
-
-    @pl.loop(0, groups)
-    def _(g):
-        attention_forward(g, sqkv, rid, kid_own, satt)
-
-    @pl.loop(0, 3)
-    def _(j):
-        at = tile_at(j)
-        res[:, at] += nn(satt[...], wq[3 * D :, at]) + sm.self_out_bias[:, at]
-
-    c_fout = fetch(3, fout_h, wq)
-    norm_forward(res, sm.self_gain, sm.self_shift, hat2, columns, 2, settled)
-
-    c_fin.wait()
+            w_at = pl.ds(pl.multiple_of(3 * D + j * TILE, TILE), TILE)
+            res[at_h, at] = tok[at_h, at].astype(F32) + nn(xatt[at_h, :], wp[:, w_at]) + sm.cross_out_bias[:, at]
+
+        @pl.when(h == NH - 1)
+        def _():
+            fetch(1, fin_h, wp)
+
+        norm_forward(res, sm.cross_gain, sm.cross_shift, hat1, columns, 1, joined, first, part_rows)
+        for part in range(3):
+            @pl.loop(0, 3)
+            def _(j):
+                at = tile_at(j)
+                y = nn(joined[at_h, :], wq[part * D : (part + 1) * D, at])
+                if part == 0:
+                    y = y + sm.self_q_bias[:, at]
+                if part == 2:
+                    y = y + sm.self_v_bias[:, at]
+                store_pairs(sqkv, y, pl.ds(pl.multiple_of(part * D + j * TILE, TILE), TILE), 2 * part_groups * h)
+
+        @pl.loop(h * part_groups, (h + 1) * part_groups)
+        def _(g):
+            attention_forward(g, sqkv, rid, kid_own, satt)
+
+        @pl.loop(0, 3)
+        def _(j):
+            at = tile_at(j)
+            res[at_h, at] += nn(satt[at_h, :], wq[3 * D :, at]) + sm.self_out_bias[:, at]
+
+        @pl.when(h == NH - 1)
+        def _():
+            fetch(3, fout_h, wq)
+
+        norm_forward(res, sm.self_gain, sm.self_shift, hat2, columns, 2, settled, first, part_rows)
+
+    pltpu.make_async_copy(fin_h, wp, sems.at[1]).wait()
 
     @pl.loop(0, FF // TILE)
     def _(j):
@@ -413,18 +456,18 @@
         x = nn(settled[...], wp[:, at]) + sm.ffn_in_bias[:, at]
         half = 0.5 * (1.0 + lax.erf(x * (0.5**0.5)))
         active[:, at] = (x * half).astype(BF)
-        inner[:, at] = (half + x * jnp.exp(-0.5 * x * x) * 0.3989422804014327).astype(BF)
-
-    c_fout.wait()
+        inner[:, at] = x.astype(BF)
+
+    pltpu.make_async_copy(fout_h, wq, sems.at[3]).wait()
 
     @pl.loop(0, 3)
     def _(j):
         at = tile_at(j)
         res[:, at] += nn(active[...], wq[:, at]) + sm.ffn_out_bias[:, at]
 
-    @pl.loop(0, rows // BLK)
+    @pl.loop(0, rows // LNB)
     def _(i):
-        at = tile_at(i, BLK)
+        at = tile_at(i, LNB)
         r = res[at, :]
         ok = columns[at, 0:1]
         gain = sm.ffn_gain[...]
@@ -443,8 +486,6 @@
         vec[FSHIFT : FSHIFT + 1, :] += total(dy)
         vec[FOUTB : FOUTB + 1, :] += total(low)
 
-    c_out = fetch(8, out_f, out_o)
-
     def slot_of(i):
         kind = PARTS[i][2]
         if kind == 0:
@@ -452,43 +493,72 @@
         ref = slot_a.at[i % 2]
         return ref if kind == 1 else ref.at[:, :, :, :, :, 0:D]
 
-    mv = SimpleNamespace(
-        core={}, y={}, x={}, zl={}, zh={}, yf={}, out={}, acc={}, rx={}, rza={}, rzb={}, fin={}
-    )
-    out_going, far_going = [], []
+    mv = SimpleNamespace(core={}, y={}, cut={}, yf={}, out={}, acc={}, got={}, fin={})
     if fused:
+        here = (zh, zl, x)
+
+        def late(i):
+            return [j for j in range(FIRST_CROSS, NP) if j not in BY_Y].index(i)
+
+        over = (to_zh, to_zl, to_x)
+
+        def cut(ref, places, *after):
+            return ref.at[(*(places.get(d, slice(None)) for d in range(3)), *after)]
+
         for i in range(NP):
             out, col, kind = PARTS[i]
-            n = IN_KIND[i]
-            a, width = acc[kind].at[n], KINDS[kind][1]
+            n, width = IN_KIND[i], KINDS[kind][1]
+            a = acc[kind].at[n]
             mv.core[i] = remote(slot_of(i).at[1 - core], a, s_core.at[i], r_core.at[i], to_core)
-            r_xi, r_zai, r_zbi = xr[kind].at[n], za[kind].at[n], zb[kind].at[n]
+            got = [xr[kind].at[n], za[kind].at[n], zb[kind].at[n]]
+            c = i - FIRST_CROSS
             if i in BY_Y:
-                c = i - FIRST_CROSS
                 mine = pl.ds(pl.multiple_of(side * HALF, HALF), HALF)
                 other = pl.ds(pl.multiple_of((1 - side) * HALF, HALF), HALF)
-                mv.y[i] = remote(a.at[:, :, :, :, other], yr.at[c], s_y.at[c], r_y.at[c], to_y)
+                mv.y[i] = remote(a.at[:, :, :, :, other], yr.at[BY_Y.index(i)], s_y.at[c], r_y.at[c], to_y)
                 a = a.at[:, :, :, :, mine]
-                cut = pl.ds(0, HALF)
-                r_xi, r_zai, r_zbi = r_xi.at[:, :, :, cut], r_zai.at[:, :, cut], r_zbi.at[:, cut]
+                short = pl.ds(0, HALF)
+                got = [got[0].at[:, :, :, short], got[1].at[:, :, short], got[2].at[:, short]]
                 width = HALF
-            mv.acc[i], mv.rx[i], mv.rza[i], mv.rzb[i] = a, r_xi, r_zai, r_zbi
-            mv.x[i] = remote(a.at[:, :, 1 - x], r_xi, s_x.at[i], r_x.at[i], to_x)
-            mv.zl[i] = remote(a.at[:, 1 - zl, x], r_zai, s_za.at[i], r_za.at[i], to_zl)
-            mv.zh[i] = remote(a.at[1 - zh, zl, x], r_zbi, s_zb.at[i], r_zb.at[i], to_zh)
-            f = fin[kind].at[n % 2]
+            mv.acc[i], mv.got[i] = a, got
+            places = {}
+            sems_of = ((s_x, r_x), (s_za, r_za), (s_zb, r_zb))
+            for step, d in enumerate(ORDER[i]):
+                send, recv = sems_of[step]
+                src = cut(a, {**places, d: 1 - here[d]})
+                mv.cut[step, i] = remote(src, got[step], send.at[i], recv.at[i], over[d])
+                places[d] = here[d]
             if i in BY_Y:
-                f = f.at[:, 0:HALF]
                 col0 = pl.ds(pl.multiple_of(col + side * HALF, HALF), HALF)
             else:
                 col0 = pl.ds(col, width)
-            mv.fin[i] = f
-            mv.out[i] = pltpu.make_async_copy(f, parts_o[out].at[:, col0], part_sems.at[i])
+            for place in range(2):
+                f = fin[kind].at[place]
+                if i in BY_Y:
+                    f = f.at[:, 0:HALF]
+                    mv.yf[i, place] = remote(f, parts_o[out].at[:, col0], s_yf.at[c], r_yf.at[c], to_y)
+                mv.fin[i, place] = f
+                mv.out[i, place] = pltpu.make_async_copy(f, parts_o[out].at[:, col0], part_sems.at[i])
+            if i >= FIRST_CROSS and i not in BY_Y:
+                mv.yf[i, 0] = remote(ybf.at[late(i), 0], ybf.at[late(i), 1], s_yf.at[c], r_yf.at[c], to_y)
+        leaving = ([], [], [])
+
+
+        def leave(i, value):
+            before = leaving[PARTS[i][2]]
+            place = len(before) % 2
+            if len(before) > 1:
+                gone(before[-2])
+            before.append((i, place))
+            mv.fin[i, place][...] = value
+            mv.out[i, place].start()
             if i in BY_Y:
-                mv.yf[i] = remote(f, parts_o[out].at[:, col0], s_yf.at[c], r_yf.at[c], to_y)
-            elif i >= FIRST_CROSS:
-                c = i - FIRST_CROSS
-                mv.yf[i] = remote(ybf.at[c // 2, 0], ybf.at[c // 2, 1], s_yf.at[c], r_yf.at[c], to_y)
+                mv.yf[i, place].start()
+
+        def gone(what):
+            mv.out[what].wait()
+            if what[0] in BY_Y:
+                mv.yf[what].wait_send()
 
         def t1(i):
             mv.core[i].wait_recv()
@@ -500,70 +570,57 @@
                 p, q, r = lax.div(d, 4), lax.rem(lax.div(d, 2), 2), lax.rem(d, 2)
                 a[p, q, r] = a[p, q, r] + own[core, p, q, r]
 
-            (mv.y if i in BY_Y else mv.x)[i].start()
+            (mv.y[i] if i in BY_Y else mv.cut[0, i]).start()
 
         def ty(i):
             mv.y[i].wait_recv()
-            a, c = mv.acc[i], i - FIRST_CROSS
+            a, c = mv.acc[i], BY_Y.index(i)
 
             @pl.loop(0, 8)
             def _(d):
                 p, q, r = lax.div(d, 4), lax.rem(lax.div(d, 2), 2), lax.rem(d, 2)
                 a[p, q, r] = a[p, q, r] + yr[c, p, q, r]
 
-            mv.x[i].start()
+            mv.cut[0, i].start()
 
         def t2(i):
-            mv.x[i].wait_recv()
-            a, r = mv.acc[i], mv.rx[i]
+            mv.cut[0, i].wait_recv()
+            a, r = mv.acc[i], mv.got[i][0]
+            first = ORDER[i][0]
 
             @pl.loop(0, 4)
             def _(d):
                 p, q = lax.div(d, 2), lax.rem(d, 2)
-                a[p, q, x] = a[p, q, x] + r[p, q]
-
-            mv.zl[i].start()
+                at = [p, q]
+                at.insert(first, here[first])
+                at = tuple(at)
+                a[at] = a[at] + r[p, q]
+
+            mv.cut[1, i].start()
 
         def t3(i):
-            mv.zl[i].wait_recv()
-            a, r = mv.acc[i], mv.rza[i]
+            mv.cut[1, i].wait_recv()
+            a, r = mv.acc[i], mv.got[i][1]
             for p in range(2):
-                a[p, zl, x] = a[p, zl, x] + r[p]
-            mv.zh[i].start()
-
-        def room(i):
-            before = [j for j in range(i) if PARTS[j][2] == PARTS[i][2] and IN_KIND[j] == IN_KIND[i] - 2]
-            for j in before:
-                mv.out[j].wait()
-                out_going.remove(j)
-                if j in BY_Y:
-                    mv.yf[j].wait_send()
-                    far_going.remove(j)
+                at = list(here)
+                at[ORDER[i][2]] = p
+                at = tuple(at)
+                a[at] = a[at] + r[p]
+            mv.cut[2, i].start()
 
         def t4(i):
-            mv.zh[i].wait_recv()
-            whole = mv.acc[i][zh, zl, x].astype(F32) + mv.rzb[i][...].astype(F32)
+            mv.cut[2, i].wait_recv()
+            whole = mv.acc[i][zh, zl, x].astype(F32) + mv.got[i][2][...].astype(F32)
             if i >= FIRST_CROSS and i not in BY_Y:
-                ybf[(i - FIRST_CROSS) // 2, 0] = whole.astype(BF)
-                mv.yf[i].start()
-                far_going.append(i)
-                return
-            room(i)
-            mv.fin[i][...] = whole
-            mv.out[i].start()
-            out_going.append(i)
-            if i in BY_Y:
-                mv.yf[i].start()
-                far_going.append(i)
+                ybf[late(i), 0] = whole.astype(BF)
+                mv.yf[i, 0].start()
+            else:
+                leave(i, whole)
 
         def tf(i):
-            mv.yf[i].wait_recv()
+            mv.yf[i, 0].wait_recv()
             if i not in BY_Y:
-                room(i)
-                c = i - FIRST_CROSS
-                mv.fin[i][...] = ybf[c // 2, 0].astype(F32) + ybf[c // 2, 1].astype(F32)
-                mv.out[i].start()
-                out_going.append(i)
+                leave(i, ybf[late(i), 0].astype(F32) + ybf[late(i), 1].astype(F32))
 
         steps = (t1, t2, t3, t4, ty, tf)
     left = []
@@ -631,7 +688,9 @@
         def _(j):
             at = tile_at(j)
             ga = nt(cot[...], wq[at, :])
-            gi = (ga * inner[:, at].astype(F32)).astype(BF)
+            y = inner[:, at].astype(F32)
+            slope = 0.5 * (1.0 + lax.erf(y * (0.5**0.5))) + y * jnp.exp(-0.5 * y * y) * 0.3989422804014327
+            gi = (ga * slope).astype(BF)
             inner[:, at] = gi
 
         serve(20 + r)
@@ -653,6 +712,10 @@
     norm_backward(res, sm.self_gain, hat2, columns, 2, g_low, vec, SGAIN, SSHIFT, SOUTB)
     serve(31)
     weight_part(6, satt, g_low, 0)
+    for j in range(D // 128):
+        by_slot(out_f[j], out_f, j)
+        satt[:, j * 128 : (j + 1) * 128] = out_f[j].astype(BF)
+    c_out = fetch(8, satt, out_o)
     for c in c_self:
         c.wait()
 
@@ -673,7 +736,7 @@
 
     @pl.loop(0, groups)
     def _(g):
-        attention_backward(g, sqkv, gpad, rid, kid_own, gx)
+        attention_backward(g, sqkv, gpad, columns, 3, gx)
         serve_each(40, g)
 
     for part in range(3):
@@ -711,7 +774,7 @@
 
     @pl.loop(0, groups)
     def _(g):
-        attention_backward(g, xqkv, gpad, rid, kid_far, gx)
+        attention_backward(g, xqkv, gpad, columns, 4, gx)
         at = pl.ds(pl.multiple_of(g * GR, GR), GR)
         pair = gx[at, D : 3 * D]
         for j in range(3):
@@ -752,12 +815,12 @@
         res[:, at] += nt(gx[:, 0:D], wp[at, 0:D])
 
     if not fused:
-        c_back = fetch(2, g_low, back_o)
-        c_grad = fetch(0, res, grad_o)
+        for src, dst in ((g_low, back_o), (res, grad_o)):
+            for j in range(D // 128):
+                by_slot(src[:, j * 128 : (j + 1) * 128].astype(F32), out_f, j)
+                fetch(0, out_f.at[j], dst.at[:, j * 128 : (j + 1) * 128]).wait()
         for done in core_free.values():
             done()
-        c_back.wait()
-        c_grad.wait()
         c_out.wait()
         return
 
@@ -767,12 +830,12 @@
     for g in range(groups):
         back_to(g).wait()
 
-    @pl.loop(0, rows // BLK)
-    def _(i):
-        at = tile_at(i, BLK)
-        res[at, :] = res[at, :] + back[at, :].astype(F32)
-
-    c_grad = fetch(0, res, grad_o)
+    c_grad = []
+    for j in range(D // 128):
+        cols = slice(j * 128, (j + 1) * 128)
+        by_slot(res[:, cols] + back[:, cols].astype(F32), out_f, j)
+        c_grad.append(pltpu.make_async_copy(out_f.at[j], grad_o.at[:, cols], sems.at[j]))
+        c_grad[-1].start()
     serve(61)
     vec_step(2)
     serve(62)
@@ -786,19 +849,22 @@
     for i in range(NP):
         if i in BY_Y:
             mv.y[i].wait_send()
-        for m in (mv.x, mv.zl, mv.zh):
-            m[i].wait_send()
-    for i in out_going:
-        mv.out[i].wait()
-    for i in far_going:
-        mv.yf[i].wait_send()
+        for step in range(3):
+            mv.cut[step, i].wait_send()
+    for before in leaving:
+        for what in before[-2:]:
+            gone(what)
+    for i in range(FIRST_CROSS, NP):
+        if i not in BY_Y:
+            mv.yf[i, 0].wait_send()
     for v in v_at:
         v.wait_send()
     v_y.wait_send()
     for g in range(groups):
         tokens_to(g).wait_send()
     c_out.wait()
-    c_grad.wait()
+    for c in c_grad:
+        c.wait()
     assert not left
 
 
@@ -820,7 +886,7 @@
         low(FF), low(FF),
         pltpu.VMEM((rows, D), F32), low(), wide(D),
         pltpu.VMEM((2 * PAD, PAD), F32),
-        pltpu.VMEM((rows, 128), F32),
+        pltpu.VMEM((rows // PAIR * PAD, 128), F32),
         pltpu.VMEM((2, 2, 2, 2, 2, BLK, 1024), BF), pltpu.VMEM((2, 2, 2, 2, 2, 4 * BLK, TILE), BF),
         pltpu.VMEM((rows // PAIR, 1, PAD), F32), pltpu.VMEM((rows // PAIR, 1, PAD), F32),
         pltpu.VMEM((8, D), F32),
@@ -834,17 +900,17 @@
         scratch += [pltpu.VMEM((2, *KINDS[k]), F32) for k in range(3)]
         cross = NP - FIRST_CROSS
         scratch += [
-            pltpu.VMEM((cross, 2, 2, 2, BLK, HALF), BF), low(), pltpu.VMEM((10, NV, D), F32),
-            pltpu.VMEM((cross // 2, 2, BLK, D), BF),
+            pltpu.VMEM((max(len(BY_Y), 1), 2, 2, 2, BLK, HALF), BF), low(), pltpu.VMEM((10, NV, D), F32),
+            pltpu.VMEM((max(cross - len(BY_Y), 1), 2, BLK, D), BF),
             *([dma(NP)] * 8), *([dma(cross)] * 4), dma(2 * rows // GR + 5), dma(2 * rows // GR + 5),
         ]
         params.update(collective_id=0, has_side_effects=True)
     return pl.pallas_call(
         partial(body, fused),
         out_shape=[
-            jax.ShapeDtypeStruct((D // 128, rows, 128), F32),
+            jax.ShapeDtypeStruct((rows, D), BF),
             jax.ShapeDtypeStruct((rows, D), F32),
-            jax.ShapeDtypeStruct((8, 128) if fused else (rows, D), BF),
+            jax.ShapeDtypeStruct((8, 128) if fused else (rows, D), F32),
             jax.ShapeDtypeStruct((NV, D), F32),
             *out_parts,
         ],
@@ -858,29 +924,14 @@
 VECTORS = (CQB, CVB, COUTB, CGAIN, CSHIFT, SQB, SVB, SOUTB, SGAIN, SSHIFT, FOUTB, FGAIN, FSHIFT)
 
 
-def finish_body(n, copies, *refs):
-    refs = list(refs)
-
-    def take(count):
-        got = refs[:count]
-        del refs[:count]
-        return got
-
-    stream_h, grad_h, vec = take(3)
-    sums = take(copies)
-    stream_o, grad_o = take(2)
-    vectors = take(len(VECTORS))
-    (finb,) = take(1)
-    sums_o = take(copies)
-    stream, grad, wide, stream_t, grad_t, sems = take(6)
-    held = take(copies)
-    items = grad.shape[0] // LR
-    c_grad = pltpu.make_async_copy(grad_h, grad, sems.at[0])
-    c_stream = pltpu.make_async_copy(stream_h, stream, sems.at[1])
-    c_grad.start()
-    c_stream.start()
-    into = [pltpu.make_async_copy(a, b, sems.at[2 + i]) for i, (a, b) in enumerate(zip(sums, held))]
-    out = [pltpu.make_async_copy(a, b, sems.at[2 + i]) for i, (a, b) in enumerate(zip(held, sums_o))]
+def finish_body(n, *refs):
+    vec, refs = refs[0], refs[1:]
+    count = (len(refs) - len(VECTORS) - 2) // 3
+    given, refs = refs[:count], refs[count:]
+    vectors, finb, refs = refs[: len(VECTORS)], refs[len(VECTORS)], refs[len(VECTORS) + 1 :]
+    out, sems, held = refs[:count], refs[count], refs[count + 1 :]
+    into = [pltpu.make_async_copy(a, b, sems.at[i]) for i, (a, b) in enumerate(zip(given, held))]
+    away = [pltpu.make_async_copy(a, b, sems.at[i]) for i, (a, b) in enumerate(zip(held, out))]
     for c in into:
         c.start()
     me = lax.axis_index("dp")
@@ -894,54 +945,32 @@
     at = lax.broadcasted_iota(jnp.int32, v.shape, 0) == lax.div(me, a_row)
     line = jnp.broadcast_to(jnp.sum(jnp.where(at, v, 0.0), axis=0, keepdims=True), v.shape)
     finb[...] = pltpu.roll(line, lax.rem(D - lax.rem(me, a_row) * share, D), 1)[0:1, 0:share]
-    c_grad.wait()
-    for j in range(D // 128):
-        cols = slice(j * 128, (j + 1) * 128)
-        for i in range(items):
-            wide[0, j, pl.ds(i, LR, stride=items), :] = grad[i * LR : (i + 1) * LR, cols]
-        grad_t[:, cols] = wide[0, j]
-    c_grad = pltpu.make_async_copy(grad_t, grad_o, sems.at[0])
-    c_grad.start()
-    for a, b in zip(into, out):
+    for a, b in zip(into, away):
         a.wait()
         b.start()
-    c_stream.wait()
-    for j in range(D // 128):
-        cols = slice(j * 128, (j + 1) * 128)
-        for i in range(items):
-            wide[1, j, pl.ds(i, LR, stride=items), :] = stream[j, i * LR : (i + 1) * LR, :]
-        stream_t[:, cols] = wide[1, j].astype(BF)
-    c_stream = pltpu.make_async_copy(stream_t, stream_o, sems.at[1])
-    c_stream.start()
-    for c in out:
-        c.wait()
-    c_grad.wait()
-    c_stream.wait()
-
-
-def finish(n, stream, grad, vec, sums):
+    for b in away:
+        b.wait()
+
+
+def finish(n, vec, arrays):
     any_space = pl.BlockSpec(memory_space=pl.ANY)
     vmem = pl.BlockSpec(memory_space=pltpu.VMEM)
     share = D // n
     shapes = [(share,)] * 5 + [(1, share)] * 8 + [(1, FF // n)]
     return pl.pallas_call(
-        partial(finish_body, n, len(sums)),
+        partial(finish_body, n),
         out_shape=[
-            jax.ShapeDtypeStruct(grad.shape, BF),
-            jax.ShapeDtypeStruct(grad.shape, F32),
             *(jax.ShapeDtypeStruct(s, F32) for s in shapes),
-            *(jax.ShapeDtypeStruct(x.shape, F32) for x in sums),
+            *(jax.ShapeDtypeStruct(x.shape, x.dtype) for x in arrays),
         ],
-        in_specs=[any_space] * 2 + [vmem] + [any_space] * len(sums),
-        out_specs=[any_space] * 2 + [vmem] * len(shapes) + [any_space] * len(sums),
+        in_specs=[vmem] + [any_space] * len(arrays),
+        out_specs=[vmem] * len(shapes) + [any_space] * len(arrays),
         scratch_shapes=[
-            pltpu.VMEM(stream.shape, F32), pltpu.VMEM(grad.shape, F32), pltpu.VMEM((2, *stream.shape), F32),
-            pltpu.VMEM(grad.shape, BF), pltpu.VMEM(grad.shape, F32),
-            pltpu.SemaphoreType.DMA((2 + len(sums),)),
-            *(pltpu.VMEM(x.shape, F32) for x in sums),
+            pltpu.SemaphoreType.DMA((max(len(arrays), 1),)),
+            *(pltpu.VMEM(x.shape, x.dtype) for x in arrays),
         ],
         compiler_params=pltpu.CompilerParams(vmem_limit_bytes=int(63.9 * 2**20)),
-    )(stream, grad, vec, *sums)
+    )(vec, *arrays)
 
 
 def partner(block):
@@ -977,13 +1006,13 @@
     shape = a["tokens"].shape
     items = shape[1]
 
-    def by_slot(v):
+    def to_slots(v):
         return v[0].transpose(1, 0, 2).reshape(items * LR, D)
 
     def back_to_items(v):
         return v.reshape(LR, items, D).transpose(1, 0, 2).reshape(shape)
 
-    tok, cot = by_slot(a["tokens"]), by_slot(a["cotangent"])
+    tok, cot = to_slots(a["tokens"]), to_slots(a["cotangent"])
     far = tok if fused else partner(tok)
     outs = compute(
         items * LR,
@@ -994,15 +1023,15 @@
     stream, grad, back, vec = outs[:4]
     sums = outs[4:]
     if not fused:
-        grad = grad + partner(back).astype(F32)
+        grad = grad + partner(back.astype(BF)).astype(F32)
         sums, vec = reduce_parts(sums, vec)
-    done = finish(n, stream, grad, vec, sums if fused else [])
+    done = finish(n, vec, [stream, grad, *sums] if fused else [])
     if fused:
-        sums = done[16:]
+        stream, grad, *sums = done[14:]
     fout, fin, sout, sqkv, cout, cqkv = sums
-    cqb, cvb, coutb, cgain, cshift, sqb, svb, soutb, sgain, sshift, foutb, fgain, fshift, finb = done[2:16]
+    cqb, cvb, coutb, cgain, cshift, sqb, svb, soutb, sgain, sshift, foutb, fgain, fshift, finb = done[:14]
     return (
-        back_to_items(done[0]), back_to_items(done[1]),
+        back_to_items(stream), back_to_items(grad),
         cqkv, cqb, cvb, cout, coutb, cgain, cshift,
         sqkv[None], sqb, svb, sout[None], soutb, sgain, sshift,
         fin[None], finb, fout[None], foutb, fgain, fshift,

time: 196 us -> 173 us (0.88)
  Pallas kernels: 194 us -> 172 us
    pallas_call x2, Pallas kernels: 194 us -> 172 us  [the longest x1 166 us: compute(): pl.pallas_call(partial(body, fused), out_shape=[jax.ShapeDtypeStruct((row...]
where the time goes in v3:
time: 173 us; the launch traced here: 172 us
  Pallas kernels  172 us (99%)
    pallas_call x1, Pallas kernels, compute(): pl.pallas_call(partial(body, fused), out_shape=[jax.ShapeDtypeStruct((row...  166 us
    pallas_call x1, Pallas kernels, finish(): pl.pallas_call(partial(finish_body, n), out_shape=[*(jax.ShapeDtypeStruct...  5.35 us

profile of v3, /device:TPU:0, one launch (start us, length us, event | category | flops | bytes accessed | tf_op | source)
XLA Modules:
  0.0 172.4 jit_solution(8212080942067976530)
XLA Ops:
  0.7 166.2 %shard_map.390 = (bf16[576,768]{1,0:T(8,128)(2,1)}, f32[576,768]{1,0:T(8,128)}, f32[8,128]{1,0:T(8,128)}, f32[24,768]{1,0:T(8,128)}, f32[192,768]{1,0:T(8,128)},...) custom-call(bf16[576,768]{1,0:T(8,128)(2,1)} %bitcast.31, ...), custom_call_target="tpu_custom_call" | custom-call | tf_op jit(solution)/shard_map/pallas_call | solution.py:908
  166.9 5.3 %shard_map.391 = (f32[48]{0:T(128)}, f32[48]{0:T(128)}, f32[48]{0:T(128)}, f32[48]{0:T(128)}, f32[48]{0:T(128)}, /*index=5*/f32[1,48]{1,0:T(1,128)}, f32[1,48]{1...) custom-call(f32[24,768]{1,0:T(8,128)} %get-tuple-element.53.refs_0_,, ...), custom_call_target="tpu_custom_call" | custom-call | tf_op jit(solution)/shard_map/pallas_call | solution.py:960

commit v4 on v3

--- a/solution.py
+++ b/solution.py
@@ -411,11 +411,7 @@
                 store_pairs(xqkv, y, slice(j * TILE, (j + 1) * TILE), 2 * g)
             attention_forward(g, xqkv, rid, kid_far, xatt)
 
-        @pl.loop(0, 3)
-        def _(j):
-            at = tile_at(j)
-            w_at = pl.ds(pl.multiple_of(3 * D + j * TILE, TILE), TILE)
-            res[at_h, at] = tok[at_h, at].astype(F32) + nn(xatt[at_h, :], wp[:, w_at]) + sm.cross_out_bias[:, at]
+        res[at_h, :] = tok[at_h, :].astype(F32) + nn(xatt[at_h, :], wp[:, 3 * D :]) + sm.cross_out_bias[...]
 
         @pl.when(h == NH - 1)
         def _():
@@ -423,24 +419,17 @@
 
         norm_forward(res, sm.cross_gain, sm.cross_shift, hat1, columns, 1, joined, first, part_rows)
         for part in range(3):
-            @pl.loop(0, 3)
-            def _(j):
-                at = tile_at(j)
-                y = nn(joined[at_h, :], wq[part * D : (part + 1) * D, at])
-                if part == 0:
-                    y = y + sm.self_q_bias[:, at]
-                if part == 2:
-                    y = y + sm.self_v_bias[:, at]
-                store_pairs(sqkv, y, pl.ds(pl.multiple_of(part * D + j * TILE, TILE), TILE), 2 * part_groups * h)
-
-        @pl.loop(h * part_groups, (h + 1) * part_groups)
-        def _(g):
-            attention_forward(g, sqkv, rid, kid_own, satt)
-
-        @pl.loop(0, 3)
-        def _(j):
-            at = tile_at(j)
-            res[at_h, at] += nn(satt[at_h, :], wq[3 * D :, at]) + sm.self_out_bias[:, at]
+            y = nn(joined[at_h, :], wq[part * D : (part + 1) * D, :])
+            if part == 0:
+                y = y + sm.self_q_bias[...]
+            if part == 2:
+                y = y + sm.self_v_bias[...]
+            store_pairs(sqkv, y, slice(part * D, (part + 1) * D), 2 * part_groups * h)
+
+        for q in range(part_groups):
+            attention_forward(h * part_groups + q, sqkv, rid, kid_own, satt)
+
+        res[at_h, :] += nn(satt[at_h, :], wq[3 * D :, :]) + sm.self_out_bias[...]
 
         @pl.when(h == NH - 1)
         def _():
@@ -460,9 +449,8 @@
 
     pltpu.make_async_copy(fout_h, wq, sems.at[3]).wait()
 
-    @pl.loop(0, 3)
-    def _(j):
-        at = tile_at(j)
+    for j in range(3):
+        at = slice(j * TILE, (j + 1) * TILE)
         res[:, at] += nn(active[...], wq[:, at]) + sm.ffn_out_bias[:, at]
 
     @pl.loop(0, rows // LNB)
@@ -788,19 +776,17 @@
     vec[CVB : CVB + 1, :] = total(gx[:, 2 * D : 3 * D])
     if fused:
         v_at = [
-            remote(vbuf.at[j], vbuf.at[4 + j], s_m.at[2 * groups + j], r_m.at[2 * groups + j], p)
+            remote(vbuf.at[j % 2], vbuf.at[2 + j], s_m.at[2 * groups + j], r_m.at[2 * groups + j], p)
             for j, p in enumerate((to_core, to_x, to_zl, to_zh))
         ]
-        v_y = remote(vbuf.at[8], vbuf.at[9], s_m.at[2 * groups + 4], r_m.at[2 * groups + 4], to_y)
+        v_y = remote(vbuf.at[0], vbuf.at[6], s_m.at[2 * groups + 4], r_m.at[2 * groups + 4], to_y)
 
         def vec_step(j):
             v_at[j].wait_recv()
-            if j < 3:
-                vbuf[j + 1] = vbuf[j] + vbuf[4 + j]
-                v_at[j + 1].start()
-            else:
-                vbuf[8] = vbuf[3] + vbuf[7]
-                v_y.start()
+            if j > 0:
+                v_at[j - 1].wait_send()
+            vbuf[(j + 1) % 2] = vbuf[j % 2] + vbuf[2 + j]
+            (v_at[j + 1] if j < 3 else v_y).start()
 
         v_at[0].start()
     weight_part(11, tok, gx, 0)
@@ -842,8 +828,8 @@
     vec_step(3)
     serve(63)
     v_y.wait_recv()
-    vec_o[...] = vbuf[8]
-    vec_o[12:, :] = vbuf[8, 12:, :] + vbuf[9, 12:, :]
+    vec_o[...] = vbuf[0]
+    vec_o[12:, :] = vbuf[0, 12:, :] + vbuf[6, 12:, :]
     for done in core_free.values():
         done()
     for i in range(NP):
@@ -857,8 +843,7 @@
     for i in range(FIRST_CROSS, NP):
         if i not in BY_Y:
             mv.yf[i, 0].wait_send()
-    for v in v_at:
-        v.wait_send()
+    v_at[3].wait_send()
     v_y.wait_send()
     for g in range(groups):
         tokens_to(g).wait_send()
@@ -900,7 +885,7 @@
         scratch += [pltpu.VMEM((2, *KINDS[k]), F32) for k in range(3)]
         cross = NP - FIRST_CROSS
         scratch += [
-            pltpu.VMEM((max(len(BY_Y), 1), 2, 2, 2, BLK, HALF), BF), low(), pltpu.VMEM((10, NV, D), F32),
+            pltpu.VMEM((max(len(BY_Y), 1), 2, 2, 2, BLK, HALF), BF), low(), pltpu.VMEM((7, NV, D), F32),
             pltpu.VMEM((max(cross - len(BY_Y), 1), 2, BLK, D), BF),
             *([dma(NP)] * 8), *([dma(cross)] * 4), dma(2 * rows // GR + 5), dma(2 * rows // GR + 5),
         ]

time: 173 us -> 168 us (0.971)
  Pallas kernels: 172 us -> 167 us
    pallas_call x1, Pallas kernels: 166 us -> 161 us  [compute(): pl.pallas_call(partial(body, fused), out_shape=[jax.ShapeDtypeStruct((row...]
where the time goes in v4:
time: 168 us; the launch traced here: 167 us
  Pallas kernels  167 us (99%)
    pallas_call x1, Pallas kernels, compute(): pl.pallas_call(partial(body, fused), out_shape=[jax.ShapeDtypeStruct((row...  161 us
    pallas_call x1, Pallas kernels, finish(): pl.pallas_call(partial(finish_body, n), out_shape=[*(jax.ShapeDtypeStruct...  5.35 us

profile of v4, /device:TPU:0, one launch (start us, length us, event | category | flops | bytes accessed | tf_op | source)
XLA Modules:
  0.0 167.4 jit_solution(4705917238079523563)
XLA Ops:
  0.7 161.2 %shard_map.390 = (bf16[576,768]{1,0:T(8,128)(2,1)}, f32[576,768]{1,0:T(8,128)}, f32[8,128]{1,0:T(8,128)}, f32[24,768]{1,0:T(8,128)}, f32[192,768]{1,0:T(8,128)},...) custom-call(bf16[576,768]{1,0:T(8,128)(2,1)} %bitcast.31, ...), custom_call_target="tpu_custom_call" | custom-call | tf_op jit(solution)/shard_map/pallas_call | solution.py:893
  161.9 5.3 %shard_map.391 = (f32[48]{0:T(128)}, f32[48]{0:T(128)}, f32[48]{0:T(128)}, f32[48]{0:T(128)}, f32[48]{0:T(128)}, /*index=5*/f32[1,48]{1,0:T(1,128)}, f32[1,48]{1...) custom-call(f32[24,768]{1,0:T(8,128)} %get-tuple-element.53.refs_0_,, ...), custom_call_target="tpu_custom_call" | custom-call | tf_op jit(solution)/shard_map/pallas_call | solution.py:945

commit v5 on v4

--- a/solution.py
+++ b/solution.py
@@ -398,8 +398,8 @@
         first = h * part_rows
         at_h = pl.ds(pl.multiple_of(first, 16), part_rows)
 
-        @pl.loop(h * part_groups, (h + 1) * part_groups)
-        def _(g):
+        for q in range(part_groups):
+            g = h * part_groups + q
             at_g = pl.ds(pl.multiple_of(g * GR, GR), GR)
             if fused:
                 tokens_to(g).wait_recv()

time: 168 us -> 168 us (level)
  no operation moved by 1% of the time
where the time goes in v5:
time: 168 us; the launch traced here: 167 us
  Pallas kernels  167 us (99%)
    pallas_call x1, Pallas kernels, compute(): pl.pallas_call(partial(body, fused), out_shape=[jax.ShapeDtypeStruct((row...  161 us
    pallas_call x1, Pallas kernels, finish(): pl.pallas_call(partial(finish_body, n), out_shape=[*(jax.ShapeDtypeStruct...  5.35 us

profile of v5, /device:TPU:0, one launch (start us, length us, event | category | flops | bytes accessed | tf_op | source)
XLA Modules:
  0.0 167.4 jit_solution(14860960093805762846)
XLA Ops:
  0.7 161.2 %shard_map.390 = (bf16[576,768]{1,0:T(8,128)(2,1)}, f32[576,768]{1,0:T(8,128)}, f32[8,128]{1,0:T(8,128)}, f32[24,768]{1,0:T(8,128)}, f32[192,768]{1,0:T(8,128)},...) custom-call(bf16[576,768]{1,0:T(8,128)(2,1)} %bitcast.31, ...), custom_call_target="tpu_custom_call" | custom-call | tf_op jit(solution)/shard_map/pallas_call | solution.py:893
  161.9 5.3 %shard_map.391 = (f32[48]{0:T(128)}, f32[48]{0:T(128)}, f32[48]{0:T(128)}, f32[48]{0:T(128)}, f32[48]{0:T(128)}, /*index=5*/f32[1,48]{1,0:T(1,128)}, f32[1,48]{1...) custom-call(f32[24,768]{1,0:T(8,128)} %get-tuple-element.53.refs_0_,, ...), custom_call_target="tpu_custom_call" | custom-call | tf_op jit(solution)/shard_map/pallas_call | solution.py:945
